TPU v7x, 32 devices: a whole 2x2x4 slice. The times are simulated.
32 devices in a mesh: ctx: 16 (over z, y, x), head: 2 (over core).
Axes of the slice: x: 2, y: 2, z: 4, core: 2. Of those that a mesh axis runs over, the one named last changes fastest.
Arguments:
- document_query: bfloat16 [4096, 8192], P('ctx', 'head'), may hold values from -6 to 6
- document_keys: bfloat16 [4096, 1024], P('ctx', 'head'), may hold values from -4 to 4
- document_values: bfloat16 [4096, 1024], P('ctx', 'head'), may hold values from -6 to 6
- question_query: bfloat16 [128, 8192], P(None, 'head'), may hold values from -10 to 10
- prompt_keys: bfloat16 [128, 1024], P(None, 'head'), may hold values from -6 to 6
- prompt_values: bfloat16 [128, 1024], P(None, 'head'), may hold values from -6 to 6
- out_weight: bfloat16 [8192, 8192], P('head', 'ctx'), may hold values from -0.0625 to 0.0625
Outputs:
- doc_attention: bfloat16 [4096, 8192], P('ctx', 'head')
- question_out: bfloat16 [128, 8192], P('head', 'ctx')
All inputs are finite; a program needn't handle non-finite values.
Results may differ from a plain program's by a relative error of at most 0.014.
Values may be sent and summed in bfloat16 or wider, within the bound.
No kernel may reach another device: no remote copies, remote signals or barrier semaphores. Data moves between devices by JAX's collectives and lax.ppermute only.
A program may use at most 64 MiB of HBM per device.

v0:
```python
import functools
import math

import jax
import jax.numpy as jnp
from jax import lax
from jax.experimental import pallas as pl
from jax.experimental.pallas import tpu as pltpu
from jax.sharding import PartitionSpec as P

QUERY_HEADS = 64
KEY_VALUE_HEADS = 8
HEAD_SIZE = 128
GROUP_WIDTH = QUERY_HEADS // KEY_VALUE_HEADS
FACTOR = HEAD_SIZE**-0.5
LOG2E = math.log2(math.e)
NEG_INF = float("-inf")
STAT_ROWS = 16
VMEM = pl.BlockSpec(memory_space=pltpu.VMEM)
ANY = pl.BlockSpec(memory_space=pl.ANY)
SMEM = pl.BlockSpec(memory_space=pltpu.SMEM)
PARAMS = pltpu.CompilerParams(vmem_limit_bytes=32 * 1024 * 1024)


def dot_nt(left, right):
    return lax.dot_general(
        left, right, (((1,), (1,)), ((), ())), preferred_element_type=jnp.float32
    )


def dot_nn(left, right):
    return jnp.dot(left, right, preferred_element_type=jnp.float32)


def with_ones(values):
    return jnp.concatenate([values, jnp.ones_like(values)], axis=1)


def columns(index, width):
    return pl.ds(pl.multiple_of(index * width, width), width)


def in_hbm(values):
    return pltpu.with_memory_space_constraint(values, pltpu.MemorySpace.HBM)


def cut_pieces(place, keys, values, group, question=()):
    token_count = keys.shape[0]

    def kernel(place_ref, keys_ref, values_ref, *refs):
        question_refs, refs = refs[: len(question)], refs[len(question) :]
        pieces, cuts, sems = refs[:group], refs[group:-1], refs[-1]
        pairs = []
        for step, piece in enumerate(pieces):
            cut = columns(place_ref[0] ^ step, HEAD_SIZE)
            for half, source in enumerate((keys_ref, values_ref)):
                pairs.append((source.at[:, cut], piece.at[pl.ds(half * token_count, token_count)]))
        for source, target in zip(question_refs, cuts):
            pairs.append((source.at[:, columns(place_ref[0], target.shape[1])], target))
        copies = [
            pltpu.make_async_copy(source, target, sems.at[i])
            for i, (source, target) in enumerate(pairs)
        ]
        for copy in copies:
            copy.start()
        for copy in copies:
            copy.wait()

    shapes = [jax.ShapeDtypeStruct((2 * token_count, HEAD_SIZE), keys.dtype)] * group + [
        jax.ShapeDtypeStruct((array.shape[0], array.shape[1] // group), array.dtype)
        for array in question
    ]
    return pl.pallas_call(
        kernel,
        out_shape=shapes,
        in_specs=[SMEM] + [ANY] * (2 + len(question)),
        out_specs=[ANY] * len(shapes),
        scratch_shapes=[pltpu.SemaphoreType.DMA((len(shapes) + group,))],
        compiler_params=PARAMS,
        name="cut_pieces",
    )(place, in_hbm(keys), in_hbm(values), *map(in_hbm, question))


def question_parts(place, query, own_keys, own_values, pieces, ring):
    group = len(pieces)
    token_count = pieces[0].shape[0] // 2
    row_count, key_count = query.shape[0], own_keys.shape[0]
    unit_heads = query.shape[1] // (HEAD_SIZE * ring)
    unit_columns = unit_heads * HEAD_SIZE
    unit_rows = unit_heads * row_count
    out_shape = (unit_rows + STAT_ROWS, HEAD_SIZE)

    def kernel(place_ref, query_ref, own_keys_ref, own_values_ref, *refs):
        piece_refs, outs = refs[:group], refs[group:]
        all_keys = jnp.concatenate([piece[:token_count] for piece in piece_refs], axis=0)
        all_values = with_ones(jnp.concatenate([piece[token_count:] for piece in piece_refs], axis=0))
        own_keys, own_values = own_keys_ref[...], with_ones(own_values_ref[...])
        lanes = lax.broadcasted_iota(jnp.int32, (row_count, HEAD_SIZE), 1)
        stat_ids = lax.broadcasted_iota(jnp.int32, (STAT_ROWS, row_count), 0)
        visible = lax.broadcasted_iota(jnp.int32, (row_count, key_count), 0) >= (
            lax.broadcasted_iota(jnp.int32, (row_count, key_count), 1)
        )
        visible = jnp.concatenate([visible] * unit_heads, axis=0)
        for step, out in enumerate(outs):
            heads = query_ref[:, columns(place_ref[1] ^ step, unit_columns)]
            queries = jnp.concatenate(
                [heads[:, i * HEAD_SIZE : (i + 1) * HEAD_SIZE] for i in range(unit_heads)], axis=0
            )
            scores, values = dot_nt(queries, all_keys), all_values
            if step == 0:
                own_scores = jnp.where(visible, dot_nt(queries, own_keys), NEG_INF)
                scores = jnp.concatenate([scores, own_scores], axis=1)
                values = jnp.concatenate([values, own_values], axis=0)
            top = scores.max(axis=1, keepdims=True) * FACTOR
            top = top.astype(jnp.bfloat16).astype(jnp.float32)
            weights = jnp.exp2(scores * (FACTOR * LOG2E) - top * LOG2E)
            sums = dot_nn(weights.astype(jnp.bfloat16), values)
            out[:unit_rows] = sums[:, :HEAD_SIZE].astype(jnp.bfloat16)
            totals = sums[:, HEAD_SIZE:]
            stats = jnp.zeros((STAT_ROWS, row_count), jnp.float32)
            for i in range(unit_heads):
                rows = slice(i * row_count, (i + 1) * row_count)
                flipped = jnp.where(lanes < HEAD_SIZE // 2, top[rows], totals[rows]).T
                total = flipped[HEAD_SIZE // 2 : HEAD_SIZE // 2 + 1]
                high = total.astype(jnp.bfloat16).astype(jnp.float32)
                for j, value in enumerate((flipped[:1], high, total - high)):
                    stats = jnp.where(stat_ids == 3 * i + j, value, stats)
            out[unit_rows:] = stats.astype(jnp.bfloat16)

    return pl.pallas_call(
        kernel,
        out_shape=[jax.ShapeDtypeStruct(out_shape, jnp.bfloat16)] * ring,
        in_specs=[SMEM] + [VMEM] * (3 + group),
        out_specs=[VMEM] * ring,
        compiler_params=PARAMS,
        name="question_parts",
    )(place, query, own_keys, own_values, *pieces)


def merge_parts(parts, row_count):
    unit_rows = parts[0].shape[0] - STAT_ROWS
    unit_heads = unit_rows // row_count

    def kernel(*refs):
        part_refs, out = refs[:-1], refs[-1]
        stats = [part[unit_rows:].astype(jnp.float32).T for part in part_refs]
        for i in range(unit_heads):
            rows = slice(i * row_count, (i + 1) * row_count)
            tops = [stat[:, 3 * i : 3 * i + 1] for stat in stats]
            totals = [stat[:, 3 * i + 1 : 3 * i + 2] + stat[:, 3 * i + 2 : 3 * i + 3] for stat in stats]
            row_top = functools.reduce(jnp.maximum, tops)
            scales = [jnp.exp(top - row_top) for top in tops]
            total = sum(scale * value for scale, value in zip(scales, totals))
            merged = sum(
                scale * part[rows].astype(jnp.float32) for scale, part in zip(scales, part_refs)
            )
            out[rows] = (merged / total).astype(jnp.bfloat16)

    return pl.pallas_call(
        kernel,
        out_shape=jax.ShapeDtypeStruct((unit_rows, HEAD_SIZE), jnp.bfloat16),
        in_specs=[VMEM] * len(parts),
        out_specs=VMEM,
        compiler_params=PARAMS,
        name="merge_parts",
    )(*parts)


def project(blocks, chunks, weight, row_count, unit_heads, splits, own_split):
    depth, width = unit_heads * HEAD_SIZE, weight.shape[1]
    arrays, spots = [], []
    for array, start in chunks:
        if not any(array is other for other in arrays):
            arrays.append(array)
        spots.append((next(i for i, other in enumerate(arrays) if other is array), start))

    def kernel(blocks_ref, split_ref, weight_ref, *refs):
        array_refs, outs, total_ref = refs[: len(arrays)], refs[len(arrays) : -1], refs[-1]
        total = None
        for at, (which, start) in enumerate(spots):
            rows = jnp.concatenate(
                [
                    array_refs[which][start + i * row_count : start + (i + 1) * row_count]
                    for i in range(unit_heads)
                ],
                axis=1,
            )
            block = weight_ref[pl.ds(pl.multiple_of(blocks_ref[at] * depth, depth), depth)]
            term = dot_nn(rows, block)
            total = term if total is None else total + term
        total_ref[...] = total
        span = row_count // splits
        for step, out in enumerate(outs):
            start = pl.multiple_of((split_ref[0] ^ step) * span, span)
            out[...] = total_ref[pl.ds(start, span)].astype(out.dtype)

    return pl.pallas_call(
        kernel,
        out_shape=[
            jax.ShapeDtypeStruct(
                (row_count // splits, width), jnp.bfloat16 if step else jnp.float32
            )
            for step in range(splits)
        ],
        in_specs=[SMEM, SMEM, VMEM] + [VMEM] * len(arrays),
        out_specs=[VMEM] * splits,
        scratch_shapes=[pltpu.VMEM((row_count, width), jnp.float32)],
        compiler_params=PARAMS,
        name="project",
    )(blocks, own_split, weight, *arrays)


def document_heads(place, query, steps, own, anchors, written=None, weight=None):
    group = len(steps)
    token_count = query.shape[0]
    step_columns = GROUP_WIDTH * HEAD_SIZE
    scale = FACTOR * LOG2E
    extra = [array for array in (written, weight) if array is not None]

    def kernel(place_ref, query_ref, *refs):
        own_refs, anchor_refs = refs[:group], refs[group : 2 * group]
        extra_refs, refs = refs[2 * group :][: len(extra)], refs[2 * group + len(extra) :]
        out, refs = refs[0], refs[1:]
        bring = None
        if weight is not None:
            bring = pltpu.make_async_copy(extra_refs[-1], refs[0], refs[-1])
            refs = refs[1:]
        queries_ref, held, query_sems, sems = refs[:4]
        cuts = [columns(place_ref[0] ^ step, step_columns) for step in steps]
        fetches = [
            pltpu.make_async_copy(
                query_ref.at[:, cuts[step]], queries_ref.at[step], query_sems.at[step]
            )
            for step in range(group)
        ]
        for fetch in fetches:
            fetch.start()
        after_anchor = place_ref[1] > 0
        visible = lax.broadcasted_iota(jnp.int32, (token_count, token_count), 0) >= (
            lax.broadcasted_iota(jnp.int32, (token_count, token_count), 1)
        )
        copies = []
        for step in range(group):
            if step == 0:
                fetches[0].wait()
            if step == 1:
                for fetch in fetches[1:]:
                    fetch.wait()
                if bring is not None:
                    bring.start()
            pair = (anchor_refs[step], own_refs[step])
            all_keys = jnp.concatenate([ref[:token_count] for ref in pair], axis=0)
            all_values = with_ones(
                jnp.concatenate([ref[token_count : 2 * token_count] for ref in pair], axis=0)
            )
            for head in range(GROUP_WIDTH):
                spot = slice(head * HEAD_SIZE, (head + 1) * HEAD_SIZE)
                scores = dot_nt(queries_ref[step, :, spot], all_keys)
                anchor_scores = scores[:, :token_count]
                own_scores = jnp.where(visible, scores[:, token_count:], NEG_INF)
                own_top = own_scores.max(axis=1, keepdims=True)
                anchor_top = anchor_scores.max(axis=1, keepdims=True)
                top = jnp.where(after_anchor, jnp.maximum(own_top, anchor_top), own_top) * scale
                anchor_shift = jnp.where(after_anchor, top, 1e30)
                anchor_exp = jnp.exp2(anchor_scores * scale - anchor_shift).astype(jnp.bfloat16)
                own_exp = jnp.exp2(own_scores * scale - top).astype(jnp.bfloat16)
                mixture = dot_nn(jnp.concatenate([anchor_exp, own_exp], axis=1), all_values)
                held[step, :, spot] = (mixture[:, :HEAD_SIZE] / mixture[:, HEAD_SIZE:]).astype(
                    held.dtype
                )
            copies.append(
                pltpu.make_async_copy(held.at[step], out.at[:, cuts[step]], sems.at[step])
            )
            copies[-1].start()
        for copy in copies:
            copy.wait()
        if bring is not None:
            bring.wait()

    out_shape = [jax.ShapeDtypeStruct(query.shape, query.dtype)]
    if weight is not None:
        out_shape.append(jax.ShapeDtypeStruct(weight.shape, weight.dtype))
    return pl.pallas_call(
        kernel,
        out_shape=out_shape,
        in_specs=[SMEM, ANY] + [VMEM] * (2 * group) + [ANY] * len(extra),
        out_specs=[ANY] * len(out_shape),
        input_output_aliases={} if written is None else {2 + 2 * group: 0},
        scratch_shapes=[
            pltpu.VMEM((group, token_count, step_columns), query.dtype),
            pltpu.VMEM((group, token_count, step_columns), query.dtype),
            pltpu.SemaphoreType.DMA((group,)),
            pltpu.SemaphoreType.DMA((group,)),
            pltpu.SemaphoreType.DMA,
        ],
        compiler_params=PARAMS,
        name="document_heads",
    )(place, in_hbm(query), *own, *anchors, *map(in_hbm, extra))


def joined(*scalars):
    return jnp.stack([jnp.asarray(scalar, jnp.int32) for scalar in scalars])


def swapped(values, axis, size, step):
    return lax.ppermute(values, axis, [(place, place ^ step) for place in range(size)])


def question_by_reduction(query, keys, values, prompt_keys, prompt_values, weight):
    row_count = query.shape[0]
    kv_total = keys.shape[1] // HEAD_SIZE
    queries = query.reshape(row_count, kv_total, GROUP_WIDTH, HEAD_SIZE)

    def part(key_block, value_block, visible):
        key_block = key_block.reshape(-1, kv_total, HEAD_SIZE)
        value_block = value_block.reshape(-1, kv_total, HEAD_SIZE)
        scores = FACTOR * jnp.einsum(
            "qhgd,khd->hgqk", queries, key_block, preferred_element_type=jnp.float32
        )
        if visible is not None:
            scores = jnp.where(visible, scores, NEG_INF)
        top = scores.max(axis=3, keepdims=True)
        weights = jnp.exp(scores - top)
        sums = jnp.einsum(
            "hgqk,khd->hgqd",
            weights.astype(jnp.bfloat16),
            value_block,
            preferred_element_type=jnp.float32,
        )
        return top, weights.sum(axis=3, keepdims=True), sums

    ids = jnp.arange(row_count, dtype=jnp.int32)
    block_top, block_total, block_sums = part(keys, values, None)
    self_top, self_total, self_sums = part(prompt_keys, prompt_values, ids[:, None] >= ids[None, :])
    row_top = jnp.maximum(lax.pmax(block_top, "ctx"), self_top)
    scale = jnp.exp(block_top - row_top)
    total, sums = lax.psum((block_total * scale, block_sums * scale), "ctx")
    self_scale = jnp.exp(self_top - row_top)
    attention = (sums + self_sums * self_scale) / (total + self_total * self_scale)
    attention = attention.astype(jnp.bfloat16).transpose(2, 0, 1, 3).reshape(row_count, -1)
    return lax.psum_scatter(
        dot_nn(attention, weight).astype(jnp.bfloat16), "head", scatter_dimension=0, tiled=True
    )


def local(
    ctx_size,
    head_size,
    document_query,
    document_keys,
    document_values,
    question_query,
    prompt_keys,
    prompt_values,
    out_weight,
):
    group = document_keys.shape[1] // HEAD_SIZE
    ring = ctx_size // group
    row_count = question_query.shape[0]
    head_total = question_query.shape[1] // HEAD_SIZE
    position = lax.axis_index("ctx")
    member, turn = position % group, position // group
    place = joined(member, turn)

    def in_group(values, step):
        return swapped(values, "ctx", ctx_size, step)

    def in_ring(values, step):
        return swapped(values, "ctx", ctx_size, step * group)

    whole_units = head_total % ctx_size == 0
    question = (question_query, prompt_keys, prompt_values) if whole_units else ()
    cuts = cut_pieces(place, document_keys, document_values, group, question)
    pieces, question = cuts[:group], cuts[group:]
    own_pieces = pieces
    pieces = [pieces[0]] + [in_group(pieces[step], step) for step in range(1, group)]

    anchor = lax.select_n(member, *pieces) if group > 1 else pieces[0]

    def sent_on(anchor, reach):
        pairs = [
            (turn_at * group + at, (turn_at + reach) * group + at)
            for turn_at in range(0, ring, 2 * reach)
            for at in range(group)
        ]
        arrived = lax.ppermute(anchor, "ctx", pairs)
        return jnp.where(turn % (2 * reach) == reach, arrived, anchor)

    spot = joined(member, position)

    reach = ring // 2
    if not whole_units:
        while reach:
            anchor = sent_on(anchor, reach)
            reach //= 2
        anchors = [anchor] + [in_group(anchor, step) for step in range(1, group)]
        doc_attention = document_heads(
            spot, document_query, range(group), own_pieces, anchors
        )[0]
        return doc_attention, question_by_reduction(
            question_query, document_keys, document_values, prompt_keys, prompt_values, out_weight
        )

    unit_heads = head_total // ctx_size
    parts = question_parts(place, *question, pieces, ring)
    parts = [parts[0]] + [in_ring(parts[step], step) for step in range(1, ring)]
    while reach > 1:
        anchor = sent_on(anchor, reach)
        reach //= 2
    parts, anchor = lax.optimization_barrier((parts, anchor))
    attention = merge_parts(parts, row_count)
    if reach:
        anchor = sent_on(anchor, reach)
    shards = [attention] + [in_ring(attention, step) for step in range(1, ring)]

    chunks = [((0, step), shards[step], 0) for step in range(ring)]
    both = jnp.concatenate([anchor, attention], axis=0)
    passed = jnp.concatenate(shards[1:], axis=0)
    beside = [in_group(both, step) for step in range(1, group)]
    far = [in_group(passed, step) for step in range(1, group)]
    anchors = [anchor] + beside
    for member_step in range(1, group):
        chunks.append(((member_step, 0), beside[member_step - 1], anchor.shape[0]))
        for step in range(1, ring):
            chunks.append(
                ((member_step, step), far[member_step - 1], (step - 1) * attention.shape[0])
            )

    doc_attention, half = None, max(1, group // 2)
    for steps in (range(half), range(half, group)):
        if steps:
            doc_attention, *brought = document_heads(
                spot,
                document_query,
                steps,
                [own_pieces[step] for step in steps],
                [anchors[step] for step in steps],
                doc_attention,
                out_weight if steps[-1] == group - 1 else None,
            )
    (near_weight,) = brought
    blocks = [
        (member ^ member_step) * ring + (turn ^ step) for (member_step, step), _, _ in chunks
    ]
    shares = project(
        joined(*blocks),
        [(array, start) for _, array, start in chunks],
        near_weight,
        row_count,
        unit_heads,
        head_size,
        joined(lax.axis_index("head")),
    )
    question_out = shares[0]
    for step in range(1, head_size):
        question_out = question_out + swapped(shares[step], "head", head_size, step).astype(
            jnp.float32
        )
    return doc_attention, question_out.astype(jnp.bfloat16)


def solution(mesh):
    placed = (
        P("ctx", "head"),
        P("ctx", "head"),
        P("ctx", "head"),
        P(None, "head"),
        P(None, "head"),
        P(None, "head"),
        P("head", "ctx"),
    )
    return jax.shard_map(
        functools.partial(local, mesh.shape["ctx"], mesh.shape["head"]),
        mesh=mesh,
        in_specs=placed,
        out_specs=(P("ctx", "head"), P("head", "ctx")),
        check_vma=False,
    )
```

profile of v0, /device:TPU:1, one launch (start us, length us, event | category | flops | bytes accessed | tf_op | source)
XLA Modules:
  0.0 58.8 jit_solution(17221771948763931645)
XLA Ops:
  0.7 0.1 pad_add_fusion.1.place_ref
  0.7 1.9 %cut_pieces.1 = (bf16[512,128]{1,0:T(8,128)(2,1)S(1)}, bf16[512,128]{1,0:T(8,128)(2,1)S(1)}, bf16[512,128]{1,0:T(8,128)(2,1)S(1)}, bf16[512,128]{1,0:T(8,128)(2,...) custom-call(s32[2]{0:T(128)S(1)} %pad_add_fusion.1.place_ref, ...), custom_call_target="tpu_custom_call" | custom-call | tf_op jit(solution)/shard_map/cut_pieces/pallas_call | solution.py:73
  2.6 2.1 %collective-permute-start = (bf16[512,128]{1,0:T(8,128)(2,1)S(1)}, bf16[512,128]{1,0:T(8,128)(2,1)S(1)}, u32[]{:S(2)}, u32[]{:S(2)}) collective-permute-start(bf16[512,128]{1,0:T(8,128)(2,1)S(1)} %get-tuple-element.28.refs_1_), channel_id=1, source_target_pairs={{0,2},{2,0},{4,6},{6,4},{8,10},{10,8},{12,14},{14,12},{16,18},{18,... | collective-permute-start | bytes 393224 | tf_op jit(solution)/shard_map/ppermute | solution.py:306
  4.7 1.2 %collective-permute-start.1 = (bf16[512,128]{1,0:T(8,128)(2,1)S(1)}, bf16[512,128]{1,0:T(8,128)(2,1)S(1)}, u32[]{:S(2)}, u32[]{:S(2)}) collective-permute-start(bf16[512,128]{1,0:T(8,128)(2,1)S(1)} %get-tuple-element.22.refs_0_), channel_id=1, source_target_pairs={{0,4},{2,6},{4,0},{6,2},{8,12},{10,14},{12,8},{14,10},{16,20},{18,... | collective-permute-start | bytes 393224 | tf_op jit(solution)/shard_map/ppermute | solution.py:306
  6.0 2.0 %collective-permute-done.refs_1_ = bf16[512,128]{1,0:T(8,128)(2,1)S(1)} collective-permute-done((bf16[512,128]{1,0:T(8,128)(2,1)S(1)}, bf16[512,128]{1,0:T(8,128)(2,1)S(1)}, u32[]{:S(2)}, u32[]{:S(2)}) %collective-permute-start) | collective-permute-done | bytes 131104 | tf_op jit(solution)/shard_map/ppermute | solution.py:306
  7.9 0.9 %collective-permute-done.1.refs_2_ = bf16[512,128]{1,0:T(8,128)(2,1)S(1)} collective-permute-done((bf16[512,128]{1,0:T(8,128)(2,1)S(1)}, bf16[512,128]{1,0:T(8,128)(2,1)S(1)}, u32[]{:S(2)}, u32[]{:S(2)}) %collective-permute-start.1) | collective-permute-done | bytes 131104 | tf_op jit(solution)/shard_map/ppermute | solution.py:306
  8.8 2.7 %collective-permute-done.2.refs_3_ = bf16[512,128]{1,0:T(8,128)(2,1)S(1)} collective-permute-done((bf16[512,128]{1,0:T(8,128)(2,1)S(1)}, bf16[512,128]{1,0:T(8,128)(2,1)S(1)}, u32[]{:S(2)}, u32[]{:S(2)}) %collective-permute-start.2) | collective-permute-done | bytes 131104 | tf_op jit(solution)/shard_map/ppermute | solution.py:306
  11.5 4.2 %collective-permute-start.6 = (bf16[512,128]{1,0:T(8,128)(2,1)S(1)}, bf16[512,128]{1,0:T(8,128)(2,1)S(1)}, u32[]{:S(2)}, u32[]{:S(2)}) collective-permute-start(bf16[512,128]{1,0:T(8,128)(2,1)S(1)} %select_select_fusion), channel_id=1, source_target_pairs={{0,16},{2,18},{4,20},{6,22},{1,17},{3,19},{5,21},{7,23}} | collective-permute-start | bytes 393224 | tf_op jit(solution)/shard_map/ppermute | solution.py:386
  15.8 2.4 %question_parts.1 = (bf16[272,128]{1,0:T(8,128)(2,1)S(1)}, bf16[272,128]{1,0:T(8,128)(2,1)S(1)}, bf16[272,128]{1,0:T(8,128)(2,1)S(1)}, bf16[272,128]{1,0:T(8,128)(2,1)S(1)}) custom-call(s32[2]{0:T(128)S(1)} %pad_add_fusion.1.place_ref, bf16[128,1024]{1,0:T(8,128)(2,1)S(1)} %get-tuple-element.24.query_ref, ...), custom_call_target="tpu_custom_call" | custom-call | tf_op jit(solution)/shard_map/question_parts/pallas_call | solution.py:130
  18.4 3.5 %collective-permute-start.5 = (bf16[272,128]{1,0:T(8,128)(2,1)S(1)}, bf16[272,128]{1,0:T(8,128)(2,1)S(1)}, u32[]{:S(2)}, u32[]{:S(2)}) collective-permute-start(bf16[272,128]{1,0:T(8,128)(2,1)S(1)} %get-tuple-element.32), channel_id=1, source_target_pairs={{0,24},{2,26},{4,28},{6,30},{8,16},{10,18},{12,20},{14,22},{16,8},... | collective-permute-start | bytes 208904 | tf_op jit(solution)/shard_map/ppermute | solution.py:306
  21.8 0.6 collective-permute-done.4.refs_2_
  22.4 2.2 %collective-permute-done.5.refs_3_ = bf16[272,128]{1,0:T(8,128)(2,1)S(1)} collective-permute-done((bf16[272,128]{1,0:T(8,128)(2,1)S(1)}, bf16[272,128]{1,0:T(8,128)(2,1)S(1)}, u32[]{:S(2)}, u32[]{:S(2)}) %collective-permute-start.5) | collective-permute-done | bytes 69664 | tf_op jit(solution)/shard_map/ppermute | solution.py:306
  24.6 0.5 merge_parts.1.refs_0_
  25.1 1.0 %collective-permute-start.11 = (bf16[256,128]{1,0:T(8,128)(2,1)S(1)}, bf16[256,128]{1,0:T(8,128)(2,1)S(1)}, u32[]{:S(2)}, u32[]{:S(2)}) collective-permute-start(bf16[256,128]{1,0:T(8,128)(2,1)S(1)} %merge_parts.1.refs_0_), channel_id=1, source_target_pairs={{0,8},{2,10},{4,12},{6,14},{8,0},{10,2},{12,4},{14,6},{16,24},{18,... | collective-permute-start | bytes 196616 | tf_op jit(solution)/shard_map/ppermute | solution.py:306
  26.1 2.4 %collective-permute-start.7 = (bf16[512,128]{1,0:T(8,128)(2,1)S(1)}, bf16[512,128]{1,0:T(8,128)(2,1)S(1)}, u32[]{:S(2)}, u32[]{:S(2)}) collective-permute-start(bf16[512,128]{1,0:T(8,128)(2,1)S(1)} %broadcast_select_fusion), channel_id=1, source_target_pairs={{0,8},{2,10},{4,12},{6,14},{16,24},{18,26},{20,28},{22,30},{1,9},{... | collective-permute-start | bytes 393224 | tf_op jit(solution)/shard_map/ppermute | solution.py:386
  28.5 2.8 %collective-permute-start.12 = (bf16[256,128]{1,0:T(8,128)(2,1)S(1)}, bf16[256,128]{1,0:T(8,128)(2,1)S(1)}, u32[]{:S(2)}, u32[]{:S(2)}) collective-permute-start(bf16[256,128]{1,0:T(8,128)(2,1)S(1)} %merge_parts.1.refs_0_), channel_id=1, source_target_pairs={{0,16},{2,18},{4,20},{6,22},{8,24},{10,26},{12,28},{14,30},{16,0},... | collective-permute-start | bytes 196616 | tf_op jit(solution)/shard_map/ppermute | solution.py:306
  31.4 1.1 %collective-permute-start.10 = (bf16[768,128]{1,0:T(8,128)(2,1)S(1)}, bf16[768,128]{1,0:T(8,128)(2,1)S(1)}, u32[]{:S(2)}, u32[]{:S(2)}) collective-permute-start(bf16[768,128]{1,0:T(8,128)(2,1)S(1)} %pad_maximum_fusion), channel_id=1, source_target_pairs={{0,2},{2,0},{4,6},{6,4},{8,10},{10,8},{12,14},{14,12},{16,18},{18,... | collective-permute-start | bytes 589832 | tf_op jit(solution)/shard_map/ppermute | solution.py:306
  32.5 0.5 collective-permute-done.12.refs_2_
  33.0 0.5 collective-permute-start.8
  33.5 1.7 %collective-permute-start.9 = (bf16[768,128]{1,0:T(8,128)(2,1)S(1)}, bf16[768,128]{1,0:T(8,128)(2,1)S(1)}, u32[]{:S(2)}, u32[]{:S(2)}) collective-permute-start(bf16[768,128]{1,0:T(8,128)(2,1)S(1)} %pad_maximum_fusion), channel_id=1, source_target_pairs={{0,6},{2,4},{4,2},{6,0},{8,14},{10,12},{12,10},{14,8},{16,22},{18,... | collective-permute-start | bytes 589832 | tf_op jit(solution)/shard_map/ppermute | solution.py:306
  35.2 1.4 %collective-permute-done.13.refs_3_ = bf16[256,128]{1,0:T(8,128)(2,1)S(1)} collective-permute-done((bf16[256,128]{1,0:T(8,128)(2,1)S(1)}, bf16[256,128]{1,0:T(8,128)(2,1)S(1)}, u32[]{:S(2)}, u32[]{:S(2)}) %collective-permute-start.13) | collective-permute-done | bytes 65568 | tf_op jit(solution)/shard_map/ppermute | solution.py:306
  36.6 1.0 %collective-permute-start.14 = (bf16[768,128]{1,0:T(8,128)(2,1)S(1)}, bf16[768,128]{1,0:T(8,128)(2,1)S(1)}, u32[]{:S(2)}, u32[]{:S(2)}) collective-permute-start(bf16[768,128]{1,0:T(8,128)(2,1)S(1)} %constant_dynamic-update-slice_fusion), channel_id=1, source_target_pairs={{0,2},{2,0},{4,6},{6,4},{8,10},{10,8},{12,14},{14,12},{16,18},{18,... | collective-permute-start | bytes 589832 | tf_op jit(solution)/shard_map/ppermute | solution.py:306
  37.6 0.5 collective-permute-start.15
  38.2 1.2 %collective-permute-start.16 = (bf16[768,128]{1,0:T(8,128)(2,1)S(1)}, bf16[768,128]{1,0:T(8,128)(2,1)S(1)}, u32[]{:S(2)}, u32[]{:S(2)}) collective-permute-start(bf16[768,128]{1,0:T(8,128)(2,1)S(1)} %constant_dynamic-update-slice_fusion), channel_id=1, source_target_pairs={{0,6},{2,4},{4,2},{6,0},{8,14},{10,12},{12,10},{14,8},{16,22},{18,... | collective-permute-start | bytes 589832 | tf_op jit(solution)/shard_map/ppermute | solution.py:306
  39.4 0.1 stack.91.blocks_ref
  39.4 0.1 pad_add_fusion.place_ref
  39.5 5.6 %document_heads.2.refs_4_ = bf16[256,4096]{1,0:T(8,128)(2,1)} custom-call(s32[2]{0:T(128)S(1)} %pad_add_fusion.place_ref, bf16[256,4096]{1,0:T(8,128)(2,1)} %query_ref.3, bf16[512,128]{1,0:T(8,128)(2,1)S(1)} %get-tuple-element.27.refs_0_, bf16[512,128]{1,0:T(8,128)(2,1)S(1)} %get-tuple-element.28.refs_1_, ...), custom_call_target="tpu_custom_call" | custom-call | tf_op jit(solution)/shard_map/document_heads/pallas_call | solution.py:283
  45.2 5.6 %document_heads.3 = (bf16[256,4096]{1,0:T(8,128)(2,1)}, bf16[4096,512]{1,0:T(8,128)(2,1)S(1)}) custom-call(s32[2]{0:T(128)S(1)} %pad_add_fusion.place_ref, bf16[256,4096]{1,0:T(8,128)(2,1)} %query_ref.3, bf16[512,128]{1,0:T(8,128)(2,1)S(1)} %get-tuple-element.22.refs_0_, ...), custom_call_target="tpu_custom_call", output_to_operand_aliasing={{0}: (6, {})} | custom-call | tf_op jit(solution)/shard_map/document_heads/pallas_call | solution.py:283
  50.9 1.3 %project.1 = (f32[64,512]{1,0:T(8,128)S(1)}, bf16[64,512]{1,0:T(8,128)(2,1)S(1)}) custom-call(s32[16]{0:T(128)S(1)} %stack.91.blocks_ref, s32[1]{0:T(128)} %bitcast.19.split_ref, bf16[4096,512]{1,0:T(8,128)(2,1)S(1)} %get-tuple-element.39.weight_ref, bf16[256,128]{1,0:T(8,128)(2,1)S(1)} %merge_parts.1.refs_0_, ...), custom_call_target="tpu_custom_call" | custom-call | tf_op jit(solution)/shard_map/project/pallas_call | solution.py:197
  52.1 5.1 %collective-permute-start.17 = (bf16[64,512]{1,0:T(8,128)(2,1)S(1)}, bf16[64,512]{1,0:T(8,128)(2,1)S(1)}, u32[]{:S(2)}, u32[]{:S(2)}) collective-permute-start(bf16[64,512]{1,0:T(8,128)(2,1)S(1)} %get-tuple-element.41), channel_id=1, source_target_pairs={{0,1},{1,0},{2,3},{3,2},{4,5},{5,4},{6,7},{7,6},{8,9},{9,8},{10,11... | collective-permute-start | bytes 196616 | tf_op jit(solution)/shard_map/ppermute | solution.py:306
  57.3 0.9 %collective-permute-done.17 = bf16[64,512]{1,0:T(8,128)(2,1)S(1)} collective-permute-done((bf16[64,512]{1,0:T(8,128)(2,1)S(1)}, bf16[64,512]{1,0:T(8,128)(2,1)S(1)}, u32[]{:S(2)}, u32[]{:S(2)}) %collective-permute-start.17) | collective-permute-done | bytes 65568 | tf_op jit(solution)/shard_map/ppermute | solution.py:306
  58.2 0.6 %add_convert_fusion = bf16[64,512]{1,0:T(8,128)(2,1)} fusion(f32[64,512]{1,0:T(8,128)S(1)} %get-tuple-element.40, bf16[64,512]{1,0:T(8,128)(2,1)S(1)} %collective-permute-done.17), kind=kLoop, calls=%fused_computation.1 | loop fusion | flops 98304 | bytes 262144 | tf_op jit(solution)/shard_map/convert_element_type | solution.py:459
  (21 shorter events, 0.3 us)
Async XLA Ops:
  2.6 5.3 %collective-permute-start = (bf16[512,128]{1,0:T(8,128)(2,1)S(1)}, bf16[512,128]{1,0:T(8,128)(2,1)S(1)}, u32[]{:S(2)}, u32[]{:S(2)}) collective-permute-start(bf16[512,128]{1,0:T(8,128)(2,1)S(1)} %get-tuple-element.28.refs_1_), channel_id=1, source_target_pairs={{0,2},{2,0},{4,6},{6,4},{8,10},{10,8},{12,14},{14,12},{16,18},{18,... | collective-permute-start | bytes 393224 | tf_op jit(solution)/shard_map/ppermute | solution.py:306
  4.7 4.1 %collective-permute-start.1 = (bf16[512,128]{1,0:T(8,128)(2,1)S(1)}, bf16[512,128]{1,0:T(8,128)(2,1)S(1)}, u32[]{:S(2)}, u32[]{:S(2)}) collective-permute-start(bf16[512,128]{1,0:T(8,128)(2,1)S(1)} %get-tuple-element.22.refs_0_), channel_id=1, source_target_pairs={{0,4},{2,6},{4,0},{6,2},{8,12},{10,14},{12,8},{14,10},{16,20},{18,... | collective-permute-start | bytes 393224 | tf_op jit(solution)/shard_map/ppermute | solution.py:306
  6.0 5.5 %collective-permute-start.2 = (bf16[512,128]{1,0:T(8,128)(2,1)S(1)}, bf16[512,128]{1,0:T(8,128)(2,1)S(1)}, u32[]{:S(2)}, u32[]{:S(2)}) collective-permute-start(bf16[512,128]{1,0:T(8,128)(2,1)S(1)} %get-tuple-element.23.refs_1_), channel_id=1, source_target_pairs={{0,6},{2,4},{4,2},{6,0},{8,14},{10,12},{12,10},{14,8},{16,22},{18,... | collective-permute-start | bytes 393224 | tf_op jit(solution)/shard_map/ppermute | solution.py:306
  11.5 10.3 %collective-permute-start.6 = (bf16[512,128]{1,0:T(8,128)(2,1)S(1)}, bf16[512,128]{1,0:T(8,128)(2,1)S(1)}, u32[]{:S(2)}, u32[]{:S(2)}) collective-permute-start(bf16[512,128]{1,0:T(8,128)(2,1)S(1)} %select_select_fusion), channel_id=1, source_target_pairs={{0,16},{2,18},{4,20},{6,22},{1,17},{3,19},{5,21},{7,23}} | collective-permute-start | bytes 393224 | tf_op jit(solution)/shard_map/ppermute | solution.py:386
  18.2 3.6 %collective-permute-start.3 = (bf16[272,128]{1,0:T(8,128)(2,1)S(1)}, bf16[272,128]{1,0:T(8,128)(2,1)S(1)}, u32[]{:S(2)}, u32[]{:S(2)}) collective-permute-start(bf16[272,128]{1,0:T(8,128)(2,1)S(1)} %get-tuple-element.30), channel_id=1, source_target_pairs={{0,8},{2,10},{4,12},{6,14},{8,0},{10,2},{12,4},{14,6},{16,24},{18,... | collective-permute-start | bytes 208904 | tf_op jit(solution)/shard_map/ppermute | solution.py:306
  18.3 4.1 %collective-permute-start.4 = (bf16[272,128]{1,0:T(8,128)(2,1)S(1)}, bf16[272,128]{1,0:T(8,128)(2,1)S(1)}, u32[]{:S(2)}, u32[]{:S(2)}) collective-permute-start(bf16[272,128]{1,0:T(8,128)(2,1)S(1)} %get-tuple-element.31), channel_id=1, source_target_pairs={{0,16},{2,18},{4,20},{6,22},{8,24},{10,26},{12,28},{14,30},{16,0},... | collective-permute-start | bytes 208904 | tf_op jit(solution)/shard_map/ppermute | solution.py:306
  18.4 6.2 %collective-permute-start.5 = (bf16[272,128]{1,0:T(8,128)(2,1)S(1)}, bf16[272,128]{1,0:T(8,128)(2,1)S(1)}, u32[]{:S(2)}, u32[]{:S(2)}) collective-permute-start(bf16[272,128]{1,0:T(8,128)(2,1)S(1)} %get-tuple-element.32), channel_id=1, source_target_pairs={{0,24},{2,26},{4,28},{6,30},{8,16},{10,18},{12,20},{14,22},{16,8},... | collective-permute-start | bytes 208904 | tf_op jit(solution)/shard_map/ppermute | solution.py:306
  25.1 6.3 %collective-permute-start.11 = (bf16[256,128]{1,0:T(8,128)(2,1)S(1)}, bf16[256,128]{1,0:T(8,128)(2,1)S(1)}, u32[]{:S(2)}, u32[]{:S(2)}) collective-permute-start(bf16[256,128]{1,0:T(8,128)(2,1)S(1)} %merge_parts.1.refs_0_), channel_id=1, source_target_pairs={{0,8},{2,10},{4,12},{6,14},{8,0},{10,2},{12,4},{14,6},{16,24},{18,... | collective-permute-start | bytes 196616 | tf_op jit(solution)/shard_map/ppermute | solution.py:306
  26.1 5.2 %collective-permute-start.7 = (bf16[512,128]{1,0:T(8,128)(2,1)S(1)}, bf16[512,128]{1,0:T(8,128)(2,1)S(1)}, u32[]{:S(2)}, u32[]{:S(2)}) collective-permute-start(bf16[512,128]{1,0:T(8,128)(2,1)S(1)} %broadcast_select_fusion), channel_id=1, source_target_pairs={{0,8},{2,10},{4,12},{6,14},{16,24},{18,26},{20,28},{22,30},{1,9},{... | collective-permute-start | bytes 393224 | tf_op jit(solution)/shard_map/ppermute | solution.py:386
  28.5 4.5 %collective-permute-start.12 = (bf16[256,128]{1,0:T(8,128)(2,1)S(1)}, bf16[256,128]{1,0:T(8,128)(2,1)S(1)}, u32[]{:S(2)}, u32[]{:S(2)}) collective-permute-start(bf16[256,128]{1,0:T(8,128)(2,1)S(1)} %merge_parts.1.refs_0_), channel_id=1, source_target_pairs={{0,16},{2,18},{4,20},{6,22},{8,24},{10,26},{12,28},{14,30},{16,0},... | collective-permute-start | bytes 196616 | tf_op jit(solution)/shard_map/ppermute | solution.py:306
  31.3 5.3 %collective-permute-start.13 = (bf16[256,128]{1,0:T(8,128)(2,1)S(1)}, bf16[256,128]{1,0:T(8,128)(2,1)S(1)}, u32[]{:S(2)}, u32[]{:S(2)}) collective-permute-start(bf16[256,128]{1,0:T(8,128)(2,1)S(1)} %merge_parts.1.refs_0_), channel_id=1, source_target_pairs={{0,24},{2,26},{4,28},{6,30},{8,16},{10,18},{12,20},{14,22},{16,8},... | collective-permute-start | bytes 196616 | tf_op jit(solution)/shard_map/ppermute | solution.py:306
  31.4 6.8 %collective-permute-start.10 = (bf16[768,128]{1,0:T(8,128)(2,1)S(1)}, bf16[768,128]{1,0:T(8,128)(2,1)S(1)}, u32[]{:S(2)}, u32[]{:S(2)}) collective-permute-start(bf16[768,128]{1,0:T(8,128)(2,1)S(1)} %pad_maximum_fusion), channel_id=1, source_target_pairs={{0,2},{2,0},{4,6},{6,4},{8,10},{10,8},{12,14},{14,12},{16,18},{18,... | collective-permute-start | bytes 589832 | tf_op jit(solution)/shard_map/ppermute | solution.py:306
  33.0 12.2 %collective-permute-start.8 = (bf16[768,128]{1,0:T(8,128)(2,1)S(1)}, bf16[768,128]{1,0:T(8,128)(2,1)S(1)}, u32[]{:S(2)}, u32[]{:S(2)}) collective-permute-start(bf16[768,128]{1,0:T(8,128)(2,1)S(1)} %pad_maximum_fusion), channel_id=1, source_target_pairs={{0,4},{2,6},{4,0},{6,2},{8,12},{10,14},{12,8},{14,10},{16,20},{18,... | collective-permute-start | bytes 589832 | tf_op jit(solution)/shard_map/ppermute | solution.py:306
  33.5 11.7 %collective-permute-start.9 = (bf16[768,128]{1,0:T(8,128)(2,1)S(1)}, bf16[768,128]{1,0:T(8,128)(2,1)S(1)}, u32[]{:S(2)}, u32[]{:S(2)}) collective-permute-start(bf16[768,128]{1,0:T(8,128)(2,1)S(1)} %pad_maximum_fusion), channel_id=1, source_target_pairs={{0,6},{2,4},{4,2},{6,0},{8,14},{10,12},{12,10},{14,8},{16,22},{18,... | collective-permute-start | bytes 589832 | tf_op jit(solution)/shard_map/ppermute | solution.py:306
  36.6 14.2 %collective-permute-start.14 = (bf16[768,128]{1,0:T(8,128)(2,1)S(1)}, bf16[768,128]{1,0:T(8,128)(2,1)S(1)}, u32[]{:S(2)}, u32[]{:S(2)}) collective-permute-start(bf16[768,128]{1,0:T(8,128)(2,1)S(1)} %constant_dynamic-update-slice_fusion), channel_id=1, source_target_pairs={{0,2},{2,0},{4,6},{6,4},{8,10},{10,8},{12,14},{14,12},{16,18},{18,... | collective-permute-start | bytes 589832 | tf_op jit(solution)/shard_map/ppermute | solution.py:306
  37.6 13.2 %collective-permute-start.15 = (bf16[768,128]{1,0:T(8,128)(2,1)S(1)}, bf16[768,128]{1,0:T(8,128)(2,1)S(1)}, u32[]{:S(2)}, u32[]{:S(2)}) collective-permute-start(bf16[768,128]{1,0:T(8,128)(2,1)S(1)} %constant_dynamic-update-slice_fusion), channel_id=1, source_target_pairs={{0,4},{2,6},{4,0},{6,2},{8,12},{10,14},{12,8},{14,10},{16,20},{18,... | collective-permute-start | bytes 589832 | tf_op jit(solution)/shard_map/ppermute | solution.py:306
  38.2 12.7 %collective-permute-start.16 = (bf16[768,128]{1,0:T(8,128)(2,1)S(1)}, bf16[768,128]{1,0:T(8,128)(2,1)S(1)}, u32[]{:S(2)}, u32[]{:S(2)}) collective-permute-start(bf16[768,128]{1,0:T(8,128)(2,1)S(1)} %constant_dynamic-update-slice_fusion), channel_id=1, source_target_pairs={{0,6},{2,4},{4,2},{6,0},{8,14},{10,12},{12,10},{14,8},{16,22},{18,... | collective-permute-start | bytes 589832 | tf_op jit(solution)/shard_map/ppermute | solution.py:306
  52.1 6.0 %collective-permute-start.17 = (bf16[64,512]{1,0:T(8,128)(2,1)S(1)}, bf16[64,512]{1,0:T(8,128)(2,1)S(1)}, u32[]{:S(2)}, u32[]{:S(2)}) collective-permute-start(bf16[64,512]{1,0:T(8,128)(2,1)S(1)} %get-tuple-element.41), channel_id=1, source_target_pairs={{0,1},{1,0},{2,3},{3,2},{4,5},{5,4},{6,7},{7,6},{8,9},{9,8},{10,11... | collective-permute-start | bytes 196616 | tf_op jit(solution)/shard_map/ppermute | solution.py:306
where the time goes:
time: 59.6 us; the launch traced here: 58.8 us
  starting transfers between devices  28.6 us (48%)
  Pallas kernels  17.3 us (29%)
  waiting for transfers between devices  11.1 us (19%)
  other arithmetic  0.87 us (1%)
  between operations  0.87 us (1%)
    ppermute x16, starting transfers between devices, swapped(): lax.ppermute(values, axis, [(place, place ^ step) for place in range(size)])  21.9 us
    pallas_call x2, Pallas kernels, document_heads(): pl.pallas_call(kernel, out_shape=out_shape, in_specs=[SMEM, ANY] + [VMEM]...  11.3 us
    ppermute x16, waiting for transfers between devices, swapped(): lax.ppermute(values, axis, [(place, place ^ step) for place in range(size)])  11.1 us
    ppermute x2, starting transfers between devices, sent_on(): arrived = lax.ppermute(anchor, 'ctx', pairs)  6.62 us
    pallas_call x1, Pallas kernels, question_parts(): pl.pallas_call(kernel, out_shape=[jax.ShapeDtypeStruct(out_shape, jnp.bfl...  2.42 us
    pallas_call x1, Pallas kernels, cut_pieces(): pl.pallas_call(kernel, out_shape=shapes, in_specs=[SMEM] + [ANY] * (2 + l...  1.88 us
    pallas_call x1, Pallas kernels, project(): pl.pallas_call(kernel, out_shape=[jax.ShapeDtypeStruct((row_count // spli...  1.28 us
  transfers between devices with their start and end apart: 18, of which 8 were waited for; matrix products, arithmetic and copies ran while one was open for 0% of the time, Pallas kernels for 23%

commit v1 on v0

--- a/solution.py
+++ b/solution.py
@@ -79,6 +79,39 @@
         compiler_params=PARAMS,
         name="cut_pieces",
     )(place, in_hbm(keys), in_hbm(values), *map(in_hbm, question))
+
+
+def query_copies(place, query_ref, steps, targets, sems):
+    return [
+        pltpu.make_async_copy(
+            query_ref.at[:, columns(place ^ step, target.shape[1])], target, sems.at[i]
+        )
+        for i, (step, target) in enumerate(zip(steps, targets))
+    ]
+
+
+def query_shapes(query, group, steps):
+    shape = (query.shape[0], query.shape[1] // group)
+    return [jax.ShapeDtypeStruct(shape, query.dtype)] * len(steps)
+
+
+def bring_queries(place, query, group, steps, piece):
+    def kernel(place_ref, query_ref, piece_ref, *refs):
+        copies = query_copies(place_ref[0], query_ref, steps, refs[:-1], refs[-1])
+        for copy in copies:
+            copy.start()
+        for copy in copies:
+            copy.wait()
+
+    return pl.pallas_call(
+        kernel,
+        out_shape=query_shapes(query, group, steps),
+        in_specs=[SMEM, ANY, ANY],
+        out_specs=[ANY] * len(steps),
+        scratch_shapes=[pltpu.SemaphoreType.DMA((len(steps),))],
+        compiler_params=PARAMS,
+        name="bring_queries",
+    )(place, in_hbm(query), piece)
 
 
 def question_parts(place, query, own_keys, own_values, pieces, ring):
@@ -210,44 +243,55 @@
     )(blocks, own_split, weight, *arrays)
 
 
-def document_heads(place, query, steps, own, anchors, written=None, weight=None):
-    group = len(steps)
-    token_count = query.shape[0]
-    step_columns = GROUP_WIDTH * HEAD_SIZE
+def document_heads(place, query, group, steps, own, anchors, near, ahead, written, weight):
+    count = len(steps)
+    token_count, total_columns = query.shape
+    step_columns = total_columns // group
     scale = FACTOR * LOG2E
-    extra = [array for array in (written, weight) if array is not None]
+    near = list(near)
+    own_fetch = () if near else steps
+    given = [array for array in (written, weight) if array is not None]
 
     def kernel(place_ref, query_ref, *refs):
-        own_refs, anchor_refs = refs[:group], refs[group : 2 * group]
-        extra_refs, refs = refs[2 * group :][: len(extra)], refs[2 * group + len(extra) :]
-        out, refs = refs[0], refs[1:]
-        bring = None
+        refs = list(refs)
+
+        def taken(number):
+            head = refs[:number]
+            del refs[:number]
+            return head
+
+        own_refs, anchor_refs, near_refs = taken(count), taken(count), taken(len(near))
+        given_refs, (out,) = taken(len(given)), taken(1)
+        ahead_refs = taken(len(ahead))
+        weight_outs = taken(1 if weight is not None else 0)
+        held, sems, weight_sem, fetch_sems, ahead_sems = taken(5)
+        if own_fetch:
+            (fetched,) = taken(1)
+            near_refs = [fetched.at[i] for i in range(count)]
+        member = place_ref[0]
+        fetches = query_copies(member, query_ref, own_fetch, near_refs, fetch_sems)
+        later = query_copies(member, query_ref, ahead, ahead_refs, ahead_sems)
         if weight is not None:
-            bring = pltpu.make_async_copy(extra_refs[-1], refs[0], refs[-1])
-            refs = refs[1:]
-        queries_ref, held, query_sems, sems = refs[:4]
-        cuts = [columns(place_ref[0] ^ step, step_columns) for step in steps]
-        fetches = [
-            pltpu.make_async_copy(
-                query_ref.at[:, cuts[step]], queries_ref.at[step], query_sems.at[step]
-            )
-            for step in range(group)
-        ]
-        for fetch in fetches:
-            fetch.start()
+            later.append(pltpu.make_async_copy(given_refs[-1], weight_outs[0], weight_sem))
+        for copy in fetches:
+            copy.start()
+        if not fetches:
+            for copy in later:
+                copy.start()
+        cuts = [columns(member ^ step, step_columns) for step in steps]
         after_anchor = place_ref[1] > 0
         visible = lax.broadcasted_iota(jnp.int32, (token_count, token_count), 0) >= (
             lax.broadcasted_iota(jnp.int32, (token_count, token_count), 1)
         )
         copies = []
-        for step in range(group):
-            if step == 0:
+        for step in range(count):
+            if fetches and step == 0:
                 fetches[0].wait()
-            if step == 1:
-                for fetch in fetches[1:]:
-                    fetch.wait()
-                if bring is not None:
-                    bring.start()
+            if fetches and step == min(1, count - 1):
+                for copy in fetches[1:]:
+                    copy.wait()
+                for copy in later:
+                    copy.start()
             pair = (anchor_refs[step], own_refs[step])
             all_keys = jnp.concatenate([ref[:token_count] for ref in pair], axis=0)
             all_values = with_ones(
@@ -255,7 +299,7 @@
             )
             for head in range(GROUP_WIDTH):
                 spot = slice(head * HEAD_SIZE, (head + 1) * HEAD_SIZE)
-                scores = dot_nt(queries_ref[step, :, spot], all_keys)
+                scores = dot_nt(near_refs[step][:, spot], all_keys)
                 anchor_scores = scores[:, :token_count]
                 own_scores = jnp.where(visible, scores[:, token_count:], NEG_INF)
                 own_top = own_scores.max(axis=1, keepdims=True)
@@ -272,30 +316,32 @@
                 pltpu.make_async_copy(held.at[step], out.at[:, cuts[step]], sems.at[step])
             )
             copies[-1].start()
-        for copy in copies:
+        for copy in copies + later:
             copy.wait()
-        if bring is not None:
-            bring.wait()
-
+
+    scratch = [
+        pltpu.VMEM((count, token_count, step_columns), query.dtype),
+        pltpu.SemaphoreType.DMA((count,)),
+        pltpu.SemaphoreType.DMA,
+        pltpu.SemaphoreType.DMA((count,)),
+        pltpu.SemaphoreType.DMA((max(1, len(ahead)),)),
+    ]
+    if own_fetch:
+        scratch.append(pltpu.VMEM((count, token_count, step_columns), query.dtype))
     out_shape = [jax.ShapeDtypeStruct(query.shape, query.dtype)]
+    out_shape += query_shapes(query, group, ahead)
     if weight is not None:
         out_shape.append(jax.ShapeDtypeStruct(weight.shape, weight.dtype))
     return pl.pallas_call(
         kernel,
         out_shape=out_shape,
-        in_specs=[SMEM, ANY] + [VMEM] * (2 * group) + [ANY] * len(extra),
+        in_specs=[SMEM, ANY] + [VMEM] * (2 * count + len(near)) + [ANY] * len(given),
         out_specs=[ANY] * len(out_shape),
-        input_output_aliases={} if written is None else {2 + 2 * group: 0},
-        scratch_shapes=[
-            pltpu.VMEM((group, token_count, step_columns), query.dtype),
-            pltpu.VMEM((group, token_count, step_columns), query.dtype),
-            pltpu.SemaphoreType.DMA((group,)),
-            pltpu.SemaphoreType.DMA((group,)),
-            pltpu.SemaphoreType.DMA,
-        ],
+        input_output_aliases={} if written is None else {2 + 2 * count + len(near): 0},
+        scratch_shapes=scratch,
         compiler_params=PARAMS,
         name="document_heads",
-    )(place, in_hbm(query), *own, *anchors, *map(in_hbm, extra))
+    )(place, in_hbm(query), *own, *anchors, *near, *map(in_hbm, given))
 
 
 def joined(*scalars):
@@ -375,6 +421,12 @@
     own_pieces = pieces
     pieces = [pieces[0]] + [in_group(pieces[step], step) for step in range(1, group)]
 
+    half = max(1, group // 2)
+    near = ()
+    if whole_units:
+        near = bring_queries(place, document_query, group, range(half), own_pieces[0])
+        pieces, near = lax.optimization_barrier((pieces, near))
+
     anchor = lax.select_n(member, *pieces) if group > 1 else pieces[0]
 
     def sent_on(anchor, reach):
@@ -395,7 +447,7 @@
             reach //= 2
         anchors = [anchor] + [in_group(anchor, step) for step in range(1, group)]
         doc_attention = document_heads(
-            spot, document_query, range(group), own_pieces, anchors
+            spot, document_query, group, range(group), own_pieces, anchors, (), (), None, None
         )[0]
         return doc_attention, question_by_reduction(
             question_query, document_keys, document_values, prompt_keys, prompt_values, out_weight
@@ -426,18 +478,22 @@
                 ((member_step, step), far[member_step - 1], (step - 1) * attention.shape[0])
             )
 
-    doc_attention, half = None, max(1, group // 2)
-    for steps in (range(half), range(half, group)):
-        if steps:
-            doc_attention, *brought = document_heads(
-                spot,
-                document_query,
-                steps,
-                [own_pieces[step] for step in steps],
-                [anchors[step] for step in steps],
-                doc_attention,
-                out_weight if steps[-1] == group - 1 else None,
-            )
+    doc_attention, calls = None, [range(half), range(half, group)][: 2 if group > 1 else 1]
+    for steps in calls:
+        last = steps[-1] == group - 1
+        doc_attention, *brought = document_heads(
+            spot,
+            document_query,
+            group,
+            steps,
+            [own_pieces[step] for step in steps],
+            [anchors[step] for step in steps],
+            near,
+            () if last else calls[1],
+            doc_attention,
+            out_weight if last else None,
+        )
+        near = brought
     (near_weight,) = brought
     blocks = [
         (member ^ member_step) * ring + (turn ^ step) for (member_step, step), _, _ in chunks

time: 59.6 us -> 57 us (0.956)
  waiting for transfers between devices: 11.1 us -> 9.32 us
  Pallas kernels: 17.3 us -> 16.5 us
    pallas_call x2, Pallas kernels: 11.3 us -> 8.7 us  [document_heads(): pl.pallas_call(kernel, out_shape=out_shape, in_specs=[SMEM, ANY] + [VMEM]...]
    ppermute x16, waiting for transfers between devices: 11.1 us -> 9.31 us  [swapped(): lax.ppermute(values, axis, [(place, place ^ step) for place in range(size)])]
    pallas_call x0 -> x1, Pallas kernels: none -> 1.76 us  [bring_queries(): pl.pallas_call(kernel, out_shape=query_shapes(query, group, steps), in_sp...]
where the time goes in v1:
time: 57 us; the launch traced here: 56.3 us
  starting transfers between devices  28.6 us (50%)
  Pallas kernels  16.5 us (29%)
  waiting for transfers between devices  9.32 us (16%)
  between operations  0.88 us (2%)
  other arithmetic  0.87 us (2%)
    ppermute x16, starting transfers between devices, swapped(): lax.ppermute(values, axis, [(place, place ^ step) for place in range(size)])  22 us
    ppermute x16, waiting for transfers between devices, swapped(): lax.ppermute(values, axis, [(place, place ^ step) for place in range(size)])  9.31 us
    pallas_call x2, Pallas kernels, document_heads(): pl.pallas_call(kernel, out_shape=out_shape, in_specs=[SMEM, ANY] + [VMEM]...  8.7 us
    ppermute x2, starting transfers between devices, sent_on(): arrived = lax.ppermute(anchor, 'ctx', pairs)  6.62 us
    pallas_call x1, Pallas kernels, question_parts(): pl.pallas_call(kernel, out_shape=[jax.ShapeDtypeStruct(out_shape, jnp.bfl...  2.42 us
    pallas_call x1, Pallas kernels, cut_pieces(): pl.pallas_call(kernel, out_shape=shapes, in_specs=[SMEM] + [ANY] * (2 + l...  1.88 us
    pallas_call x1, Pallas kernels, bring_queries(): pl.pallas_call(kernel, out_shape=query_shapes(query, group, steps), in_sp...  1.76 us
    pallas_call x1, Pallas kernels, project(): pl.pallas_call(kernel, out_shape=[jax.ShapeDtypeStruct((row_count // spli...  1.28 us
  transfers between devices with their start and end apart: 18, of which 8 were waited for; matrix products, arithmetic and copies ran while one was open for 0% of the time, Pallas kernels for 23%

profile of v1, /device:TPU:1, one launch (start us, length us, event | category | flops | bytes accessed | tf_op | source)
XLA Modules:
  0.0 56.3 jit_solution(17048880445397073739)
XLA Ops:
  0.7 1.9 %cut_pieces.1 = (bf16[512,128]{1,0:T(8,128)(2,1)S(1)}, bf16[512,128]{1,0:T(8,128)(2,1)S(1)}, bf16[512,128]{1,0:T(8,128)(2,1)S(1)}, bf16[512,128]{1,0:T(8,128)(2,...) custom-call(s32[2]{0:T(128)S(1)} %pad_add_fusion.1.place_ref, ...), custom_call_target="tpu_custom_call" | custom-call | tf_op jit(solution)/shard_map/cut_pieces/pallas_call | solution.py:73
  2.6 2.1 %collective-permute-start = (bf16[512,128]{1,0:T(8,128)(2,1)S(1)}, bf16[512,128]{1,0:T(8,128)(2,1)S(1)}, u32[]{:S(2)}, u32[]{:S(2)}) collective-permute-start(bf16[512,128]{1,0:T(8,128)(2,1)S(1)} %get-tuple-element.39.refs_1_), channel_id=1, source_target_pairs={{0,2},{2,0},{4,6},{6,4},{8,10},{10,8},{12,14},{14,12},{16,18},{18,... | collective-permute-start | bytes 393224 | tf_op jit(solution)/shard_map/ppermute | solution.py:352
  4.7 1.2 %collective-permute-start.1 = (bf16[512,128]{1,0:T(8,128)(2,1)S(1)}, bf16[512,128]{1,0:T(8,128)(2,1)S(1)}, u32[]{:S(2)}, u32[]{:S(2)}) collective-permute-start(bf16[512,128]{1,0:T(8,128)(2,1)S(1)} %get-tuple-element.33.refs_0_), channel_id=1, source_target_pairs={{0,4},{2,6},{4,0},{6,2},{8,12},{10,14},{12,8},{14,10},{16,20},{18,... | collective-permute-start | bytes 393224 | tf_op jit(solution)/shard_map/ppermute | solution.py:352
  6.0 1.8 %bring_queries.1 = (bf16[256,1024]{1,0:T(8,128)(2,1)S(1)}, bf16[256,1024]{1,0:T(8,128)(2,1)S(1)}) custom-call(s32[2]{0:T(128)S(1)} %pad_add_fusion.1.place_ref, bf16[256,4096]{1,0:T(8,128)(2,1)} %query_ref.5, bf16[512,128]{1,0:T(8,128)(2,1)S(1)} %get-tuple-element.42.piece_ref.refs_0_), custom_call_target="tpu_custom_call" | custom-call | tf_op jit(solution)/shard_map/bring_queries/pallas_call | solution.py:106
  7.8 0.2 collective-permute-done.refs_1_
  7.9 0.9 %collective-permute-done.1.refs_2_ = bf16[512,128]{1,0:T(8,128)(2,1)S(1)} collective-permute-done((bf16[512,128]{1,0:T(8,128)(2,1)S(1)}, bf16[512,128]{1,0:T(8,128)(2,1)S(1)}, u32[]{:S(2)}, u32[]{:S(2)}) %collective-permute-start.1) | collective-permute-done | bytes 131104 | tf_op jit(solution)/shard_map/ppermute | solution.py:352
  8.8 2.7 %collective-permute-done.2.refs_3_ = bf16[512,128]{1,0:T(8,128)(2,1)S(1)} collective-permute-done((bf16[512,128]{1,0:T(8,128)(2,1)S(1)}, bf16[512,128]{1,0:T(8,128)(2,1)S(1)}, u32[]{:S(2)}, u32[]{:S(2)}) %collective-permute-start.2) | collective-permute-done | bytes 131104 | tf_op jit(solution)/shard_map/ppermute | solution.py:352
  11.5 4.2 %collective-permute-start.6 = (bf16[512,128]{1,0:T(8,128)(2,1)S(1)}, bf16[512,128]{1,0:T(8,128)(2,1)S(1)}, u32[]{:S(2)}, u32[]{:S(2)}) collective-permute-start(bf16[512,128]{1,0:T(8,128)(2,1)S(1)} %select_select_fusion), channel_id=1, source_target_pairs={{0,16},{2,18},{4,20},{6,22},{1,17},{3,19},{5,21},{7,23}} | collective-permute-start | bytes 393224 | tf_op jit(solution)/shard_map/ppermute | solution.py:438
  15.8 2.4 %question_parts.1 = (bf16[272,128]{1,0:T(8,128)(2,1)S(1)}, bf16[272,128]{1,0:T(8,128)(2,1)S(1)}, bf16[272,128]{1,0:T(8,128)(2,1)S(1)}, bf16[272,128]{1,0:T(8,128)(2,1)S(1)}) custom-call(s32[2]{0:T(128)S(1)} %pad_add_fusion.1.place_ref, bf16[128,1024]{1,0:T(8,128)(2,1)S(1)} %get-tuple-element.35.query_ref, ...), custom_call_target="tpu_custom_call" | custom-call | tf_op jit(solution)/shard_map/question_parts/pallas_call | solution.py:163
  18.4 3.5 %collective-permute-start.5 = (bf16[272,128]{1,0:T(8,128)(2,1)S(1)}, bf16[272,128]{1,0:T(8,128)(2,1)S(1)}, u32[]{:S(2)}, u32[]{:S(2)}) collective-permute-start(bf16[272,128]{1,0:T(8,128)(2,1)S(1)} %get-tuple-element.49), channel_id=1, source_target_pairs={{0,24},{2,26},{4,28},{6,30},{8,16},{10,18},{12,20},{14,22},{16,8},... | collective-permute-start | bytes 208904 | tf_op jit(solution)/shard_map/ppermute | solution.py:352
  21.8 0.6 collective-permute-done.4.refs_2_
  22.4 2.2 %collective-permute-done.5.refs_3_ = bf16[272,128]{1,0:T(8,128)(2,1)S(1)} collective-permute-done((bf16[272,128]{1,0:T(8,128)(2,1)S(1)}, bf16[272,128]{1,0:T(8,128)(2,1)S(1)}, u32[]{:S(2)}, u32[]{:S(2)}) %collective-permute-start.5) | collective-permute-done | bytes 69664 | tf_op jit(solution)/shard_map/ppermute | solution.py:352
  24.6 0.5 merge_parts.1.refs_0_
  25.1 1.0 %collective-permute-start.11 = (bf16[256,128]{1,0:T(8,128)(2,1)S(1)}, bf16[256,128]{1,0:T(8,128)(2,1)S(1)}, u32[]{:S(2)}, u32[]{:S(2)}) collective-permute-start(bf16[256,128]{1,0:T(8,128)(2,1)S(1)} %merge_parts.1.refs_0_), channel_id=1, source_target_pairs={{0,8},{2,10},{4,12},{6,14},{8,0},{10,2},{12,4},{14,6},{16,24},{18,... | collective-permute-start | bytes 196616 | tf_op jit(solution)/shard_map/ppermute | solution.py:352
  26.1 2.4 %collective-permute-start.7 = (bf16[512,128]{1,0:T(8,128)(2,1)S(1)}, bf16[512,128]{1,0:T(8,128)(2,1)S(1)}, u32[]{:S(2)}, u32[]{:S(2)}) collective-permute-start(bf16[512,128]{1,0:T(8,128)(2,1)S(1)} %broadcast_select_fusion), channel_id=1, source_target_pairs={{0,8},{2,10},{4,12},{6,14},{16,24},{18,26},{20,28},{22,30},{1,9},{... | collective-permute-start | bytes 393224 | tf_op jit(solution)/shard_map/ppermute | solution.py:438
  28.5 2.8 %collective-permute-start.12 = (bf16[256,128]{1,0:T(8,128)(2,1)S(1)}, bf16[256,128]{1,0:T(8,128)(2,1)S(1)}, u32[]{:S(2)}, u32[]{:S(2)}) collective-permute-start(bf16[256,128]{1,0:T(8,128)(2,1)S(1)} %merge_parts.1.refs_0_), channel_id=1, source_target_pairs={{0,16},{2,18},{4,20},{6,22},{8,24},{10,26},{12,28},{14,30},{16,0},... | collective-permute-start | bytes 196616 | tf_op jit(solution)/shard_map/ppermute | solution.py:352
  31.4 1.1 %collective-permute-start.10 = (bf16[768,128]{1,0:T(8,128)(2,1)S(1)}, bf16[768,128]{1,0:T(8,128)(2,1)S(1)}, u32[]{:S(2)}, u32[]{:S(2)}) collective-permute-start(bf16[768,128]{1,0:T(8,128)(2,1)S(1)} %pad_maximum_fusion), channel_id=1, source_target_pairs={{0,2},{2,0},{4,6},{6,4},{8,10},{10,8},{12,14},{14,12},{16,18},{18,... | collective-permute-start | bytes 589832 | tf_op jit(solution)/shard_map/ppermute | solution.py:352
  32.5 0.5 collective-permute-done.12.refs_2_
  33.0 0.5 collective-permute-start.8
  33.5 1.7 %collective-permute-start.9 = (bf16[768,128]{1,0:T(8,128)(2,1)S(1)}, bf16[768,128]{1,0:T(8,128)(2,1)S(1)}, u32[]{:S(2)}, u32[]{:S(2)}) collective-permute-start(bf16[768,128]{1,0:T(8,128)(2,1)S(1)} %pad_maximum_fusion), channel_id=1, source_target_pairs={{0,6},{2,4},{4,2},{6,0},{8,14},{10,12},{12,10},{14,8},{16,22},{18,... | collective-permute-start | bytes 589832 | tf_op jit(solution)/shard_map/ppermute | solution.py:352
  35.2 1.4 %collective-permute-done.13.refs_3_ = bf16[256,128]{1,0:T(8,128)(2,1)S(1)} collective-permute-done((bf16[256,128]{1,0:T(8,128)(2,1)S(1)}, bf16[256,128]{1,0:T(8,128)(2,1)S(1)}, u32[]{:S(2)}, u32[]{:S(2)}) %collective-permute-start.13) | collective-permute-done | bytes 65568 | tf_op jit(solution)/shard_map/ppermute | solution.py:352
  36.6 1.0 %collective-permute-start.14 = (bf16[768,128]{1,0:T(8,128)(2,1)S(1)}, bf16[768,128]{1,0:T(8,128)(2,1)S(1)}, u32[]{:S(2)}, u32[]{:S(2)}) collective-permute-start(bf16[768,128]{1,0:T(8,128)(2,1)S(1)} %constant_dynamic-update-slice_fusion), channel_id=1, source_target_pairs={{0,2},{2,0},{4,6},{6,4},{8,10},{10,8},{12,14},{14,12},{16,18},{18,... | collective-permute-start | bytes 589832 | tf_op jit(solution)/shard_map/ppermute | solution.py:352
  37.6 0.5 collective-permute-start.15
  38.2 1.2 %collective-permute-start.16 = (bf16[768,128]{1,0:T(8,128)(2,1)S(1)}, bf16[768,128]{1,0:T(8,128)(2,1)S(1)}, u32[]{:S(2)}, u32[]{:S(2)}) collective-permute-start(bf16[768,128]{1,0:T(8,128)(2,1)S(1)} %constant_dynamic-update-slice_fusion), channel_id=1, source_target_pairs={{0,6},{2,4},{4,2},{6,0},{8,14},{10,12},{12,10},{14,8},{16,22},{18,... | collective-permute-start | bytes 589832 | tf_op jit(solution)/shard_map/ppermute | solution.py:352
  39.4 0.1 stack.91.blocks_ref
  39.4 0.1 pad_add_fusion.place_ref
  39.5 4.5 %document_heads.2 = (bf16[256,4096]{1,0:T(8,128)(2,1)}, bf16[256,1024]{1,0:T(8,128)(2,1)S(1)}, bf16[256,1024]{1,0:T(8,128)(2,1)S(1)}) custom-call(s32[2]{0:T(128)S(1)} %pad_add_fusion.place_ref, bf16[256,4096]{1,0:T(8,128)(2,1)} %query_ref.5, bf16[512,128]{1,0:T(8,128)(2,1)S(1)} %get-tuple-element.42.piece_ref.refs_0_, ...), custom_call_target="tpu_custom_call" | custom-call | tf_op jit(solution)/shard_map/document_heads/pallas_call | solution.py:335
  44.1 4.2 %document_heads.3 = (bf16[256,4096]{1,0:T(8,128)(2,1)}, bf16[4096,512]{1,0:T(8,128)(2,1)S(1)}) custom-call(s32[2]{0:T(128)S(1)} %pad_add_fusion.place_ref, bf16[256,4096]{1,0:T(8,128)(2,1)} %query_ref.5, bf16[512,128]{1,0:T(8,128)(2,1)S(1)} %get-tuple-element.33.refs_0_, ...), custom_call_target="tpu_custom_call", output_to_operand_aliasing={{0}: (8, {})} | custom-call | tf_op jit(solution)/shard_map/document_heads/pallas_call | solution.py:335
  48.3 1.3 %project.1 = (f32[64,512]{1,0:T(8,128)S(1)}, bf16[64,512]{1,0:T(8,128)(2,1)S(1)}) custom-call(s32[16]{0:T(128)S(1)} %stack.91.blocks_ref, s32[1]{0:T(128)} %bitcast.19.split_ref, bf16[4096,512]{1,0:T(8,128)(2,1)S(1)} %get-tuple-element.61.weight_ref, bf16[256,128]{1,0:T(8,128)(2,1)S(1)} %merge_parts.1.refs_0_, ...), custom_call_target="tpu_custom_call" | custom-call | tf_op jit(solution)/shard_map/project/pallas_call | solution.py:230
  49.6 5.2 %collective-permute-start.17 = (bf16[64,512]{1,0:T(8,128)(2,1)S(1)}, bf16[64,512]{1,0:T(8,128)(2,1)S(1)}, u32[]{:S(2)}, u32[]{:S(2)}) collective-permute-start(bf16[64,512]{1,0:T(8,128)(2,1)S(1)} %get-tuple-element.63), channel_id=1, source_target_pairs={{0,1},{1,0},{2,3},{3,2},{4,5},{5,4},{6,7},{7,6},{8,9},{9,8},{10,11... | collective-permute-start | bytes 196616 | tf_op jit(solution)/shard_map/ppermute | solution.py:352
  54.8 0.9 %collective-permute-done.17 = bf16[64,512]{1,0:T(8,128)(2,1)S(1)} collective-permute-done((bf16[64,512]{1,0:T(8,128)(2,1)S(1)}, bf16[64,512]{1,0:T(8,128)(2,1)S(1)}, u32[]{:S(2)}, u32[]{:S(2)}) %collective-permute-start.17) | collective-permute-done | bytes 65568 | tf_op jit(solution)/shard_map/ppermute | solution.py:352
  55.7 0.6 %add_convert_fusion = bf16[64,512]{1,0:T(8,128)(2,1)} fusion(f32[64,512]{1,0:T(8,128)S(1)} %get-tuple-element.62, bf16[64,512]{1,0:T(8,128)(2,1)S(1)} %collective-permute-done.17), kind=kLoop, calls=%fused_computation.1 | loop fusion | flops 98304 | bytes 262144 | tf_op jit(solution)/shard_map/convert_element_type | solution.py:515
  (22 shorter events, 0.4 us)
Async XLA Ops:
  2.6 5.3 %collective-permute-start = (bf16[512,128]{1,0:T(8,128)(2,1)S(1)}, bf16[512,128]{1,0:T(8,128)(2,1)S(1)}, u32[]{:S(2)}, u32[]{:S(2)}) collective-permute-start(bf16[512,128]{1,0:T(8,128)(2,1)S(1)} %get-tuple-element.39.refs_1_), channel_id=1, source_target_pairs={{0,2},{2,0},{4,6},{6,4},{8,10},{10,8},{12,14},{14,12},{16,18},{18,... | collective-permute-start | bytes 393224 | tf_op jit(solution)/shard_map/ppermute | solution.py:352
  4.7 4.1 %collective-permute-start.1 = (bf16[512,128]{1,0:T(8,128)(2,1)S(1)}, bf16[512,128]{1,0:T(8,128)(2,1)S(1)}, u32[]{:S(2)}, u32[]{:S(2)}) collective-permute-start(bf16[512,128]{1,0:T(8,128)(2,1)S(1)} %get-tuple-element.33.refs_0_), channel_id=1, source_target_pairs={{0,4},{2,6},{4,0},{6,2},{8,12},{10,14},{12,8},{14,10},{16,20},{18,... | collective-permute-start | bytes 393224 | tf_op jit(solution)/shard_map/ppermute | solution.py:352
  6.0 5.5 %collective-permute-start.2 = (bf16[512,128]{1,0:T(8,128)(2,1)S(1)}, bf16[512,128]{1,0:T(8,128)(2,1)S(1)}, u32[]{:S(2)}, u32[]{:S(2)}) collective-permute-start(bf16[512,128]{1,0:T(8,128)(2,1)S(1)} %get-tuple-element.34.refs_1_), channel_id=1, source_target_pairs={{0,6},{2,4},{4,2},{6,0},{8,14},{10,12},{12,10},{14,8},{16,22},{18,... | collective-permute-start | bytes 393224 | tf_op jit(solution)/shard_map/ppermute | solution.py:352
  11.5 10.3 %collective-permute-start.6 = (bf16[512,128]{1,0:T(8,128)(2,1)S(1)}, bf16[512,128]{1,0:T(8,128)(2,1)S(1)}, u32[]{:S(2)}, u32[]{:S(2)}) collective-permute-start(bf16[512,128]{1,0:T(8,128)(2,1)S(1)} %select_select_fusion), channel_id=1, source_target_pairs={{0,16},{2,18},{4,20},{6,22},{1,17},{3,19},{5,21},{7,23}} | collective-permute-start | bytes 393224 | tf_op jit(solution)/shard_map/ppermute | solution.py:438
  18.2 3.6 %collective-permute-start.3 = (bf16[272,128]{1,0:T(8,128)(2,1)S(1)}, bf16[272,128]{1,0:T(8,128)(2,1)S(1)}, u32[]{:S(2)}, u32[]{:S(2)}) collective-permute-start(bf16[272,128]{1,0:T(8,128)(2,1)S(1)} %get-tuple-element.47), channel_id=1, source_target_pairs={{0,8},{2,10},{4,12},{6,14},{8,0},{10,2},{12,4},{14,6},{16,24},{18,... | collective-permute-start | bytes 208904 | tf_op jit(solution)/shard_map/ppermute | solution.py:352
  18.3 4.1 %collective-permute-start.4 = (bf16[272,128]{1,0:T(8,128)(2,1)S(1)}, bf16[272,128]{1,0:T(8,128)(2,1)S(1)}, u32[]{:S(2)}, u32[]{:S(2)}) collective-permute-start(bf16[272,128]{1,0:T(8,128)(2,1)S(1)} %get-tuple-element.48), channel_id=1, source_target_pairs={{0,16},{2,18},{4,20},{6,22},{8,24},{10,26},{12,28},{14,30},{16,0},... | collective-permute-start | bytes 208904 | tf_op jit(solution)/shard_map/ppermute | solution.py:352
  18.4 6.2 %collective-permute-start.5 = (bf16[272,128]{1,0:T(8,128)(2,1)S(1)}, bf16[272,128]{1,0:T(8,128)(2,1)S(1)}, u32[]{:S(2)}, u32[]{:S(2)}) collective-permute-start(bf16[272,128]{1,0:T(8,128)(2,1)S(1)} %get-tuple-element.49), channel_id=1, source_target_pairs={{0,24},{2,26},{4,28},{6,30},{8,16},{10,18},{12,20},{14,22},{16,8},... | collective-permute-start | bytes 208904 | tf_op jit(solution)/shard_map/ppermute | solution.py:352
  25.1 6.3 %collective-permute-start.11 = (bf16[256,128]{1,0:T(8,128)(2,1)S(1)}, bf16[256,128]{1,0:T(8,128)(2,1)S(1)}, u32[]{:S(2)}, u32[]{:S(2)}) collective-permute-start(bf16[256,128]{1,0:T(8,128)(2,1)S(1)} %merge_parts.1.refs_0_), channel_id=1, source_target_pairs={{0,8},{2,10},{4,12},{6,14},{8,0},{10,2},{12,4},{14,6},{16,24},{18,... | collective-permute-start | bytes 196616 | tf_op jit(solution)/shard_map/ppermute | solution.py:352
  26.1 5.2 %collective-permute-start.7 = (bf16[512,128]{1,0:T(8,128)(2,1)S(1)}, bf16[512,128]{1,0:T(8,128)(2,1)S(1)}, u32[]{:S(2)}, u32[]{:S(2)}) collective-permute-start(bf16[512,128]{1,0:T(8,128)(2,1)S(1)} %broadcast_select_fusion), channel_id=1, source_target_pairs={{0,8},{2,10},{4,12},{6,14},{16,24},{18,26},{20,28},{22,30},{1,9},{... | collective-permute-start | bytes 393224 | tf_op jit(solution)/shard_map/ppermute | solution.py:438
  28.5 4.5 %collective-permute-start.12 = (bf16[256,128]{1,0:T(8,128)(2,1)S(1)}, bf16[256,128]{1,0:T(8,128)(2,1)S(1)}, u32[]{:S(2)}, u32[]{:S(2)}) collective-permute-start(bf16[256,128]{1,0:T(8,128)(2,1)S(1)} %merge_parts.1.refs_0_), channel_id=1, source_target_pairs={{0,16},{2,18},{4,20},{6,22},{8,24},{10,26},{12,28},{14,30},{16,0},... | collective-permute-start | bytes 196616 | tf_op jit(solution)/shard_map/ppermute | solution.py:352
  31.3 5.3 %collective-permute-start.13 = (bf16[256,128]{1,0:T(8,128)(2,1)S(1)}, bf16[256,128]{1,0:T(8,128)(2,1)S(1)}, u32[]{:S(2)}, u32[]{:S(2)}) collective-permute-start(bf16[256,128]{1,0:T(8,128)(2,1)S(1)} %merge_parts.1.refs_0_), channel_id=1, source_target_pairs={{0,24},{2,26},{4,28},{6,30},{8,16},{10,18},{12,20},{14,22},{16,8},... | collective-permute-start | bytes 196616 | tf_op jit(solution)/shard_map/ppermute | solution.py:352
  31.4 6.8 %collective-permute-start.10 = (bf16[768,128]{1,0:T(8,128)(2,1)S(1)}, bf16[768,128]{1,0:T(8,128)(2,1)S(1)}, u32[]{:S(2)}, u32[]{:S(2)}) collective-permute-start(bf16[768,128]{1,0:T(8,128)(2,1)S(1)} %pad_maximum_fusion), channel_id=1, source_target_pairs={{0,2},{2,0},{4,6},{6,4},{8,10},{10,8},{12,14},{14,12},{16,18},{18,... | collective-permute-start | bytes 589832 | tf_op jit(solution)/shard_map/ppermute | solution.py:352
  33.0 11.0 %collective-permute-start.8 = (bf16[768,128]{1,0:T(8,128)(2,1)S(1)}, bf16[768,128]{1,0:T(8,128)(2,1)S(1)}, u32[]{:S(2)}, u32[]{:S(2)}) collective-permute-start(bf16[768,128]{1,0:T(8,128)(2,1)S(1)} %pad_maximum_fusion), channel_id=1, source_target_pairs={{0,4},{2,6},{4,0},{6,2},{8,12},{10,14},{12,8},{14,10},{16,20},{18,... | collective-permute-start | bytes 589832 | tf_op jit(solution)/shard_map/ppermute | solution.py:352
  33.5 10.6 %collective-permute-start.9 = (bf16[768,128]{1,0:T(8,128)(2,1)S(1)}, bf16[768,128]{1,0:T(8,128)(2,1)S(1)}, u32[]{:S(2)}, u32[]{:S(2)}) collective-permute-start(bf16[768,128]{1,0:T(8,128)(2,1)S(1)} %pad_maximum_fusion), channel_id=1, source_target_pairs={{0,6},{2,4},{4,2},{6,0},{8,14},{10,12},{12,10},{14,8},{16,22},{18,... | collective-permute-start | bytes 589832 | tf_op jit(solution)/shard_map/ppermute | solution.py:352
  36.6 11.6 %collective-permute-start.14 = (bf16[768,128]{1,0:T(8,128)(2,1)S(1)}, bf16[768,128]{1,0:T(8,128)(2,1)S(1)}, u32[]{:S(2)}, u32[]{:S(2)}) collective-permute-start(bf16[768,128]{1,0:T(8,128)(2,1)S(1)} %constant_dynamic-update-slice_fusion), channel_id=1, source_target_pairs={{0,2},{2,0},{4,6},{6,4},{8,10},{10,8},{12,14},{14,12},{16,18},{18,... | collective-permute-start | bytes 589832 | tf_op jit(solution)/shard_map/ppermute | solution.py:352
  37.6 10.6 %collective-permute-start.15 = (bf16[768,128]{1,0:T(8,128)(2,1)S(1)}, bf16[768,128]{1,0:T(8,128)(2,1)S(1)}, u32[]{:S(2)}, u32[]{:S(2)}) collective-permute-start(bf16[768,128]{1,0:T(8,128)(2,1)S(1)} %constant_dynamic-update-slice_fusion), channel_id=1, source_target_pairs={{0,4},{2,6},{4,0},{6,2},{8,12},{10,14},{12,8},{14,10},{16,20},{18,... | collective-permute-start | bytes 589832 | tf_op jit(solution)/shard_map/ppermute | solution.py:352
  38.2 10.1 %collective-permute-start.16 = (bf16[768,128]{1,0:T(8,128)(2,1)S(1)}, bf16[768,128]{1,0:T(8,128)(2,1)S(1)}, u32[]{:S(2)}, u32[]{:S(2)}) collective-permute-start(bf16[768,128]{1,0:T(8,128)(2,1)S(1)} %constant_dynamic-update-slice_fusion), channel_id=1, source_target_pairs={{0,6},{2,4},{4,2},{6,0},{8,14},{10,12},{12,10},{14,8},{16,22},{18,... | collective-permute-start | bytes 589832 | tf_op jit(solution)/shard_map/ppermute | solution.py:352
  49.6 6.1 %collective-permute-start.17 = (bf16[64,512]{1,0:T(8,128)(2,1)S(1)}, bf16[64,512]{1,0:T(8,128)(2,1)S(1)}, u32[]{:S(2)}, u32[]{:S(2)}) collective-permute-start(bf16[64,512]{1,0:T(8,128)(2,1)S(1)} %get-tuple-element.63), channel_id=1, source_target_pairs={{0,1},{1,0},{2,3},{3,2},{4,5},{5,4},{6,7},{7,6},{8,9},{9,8},{10,11... | collective-permute-start | bytes 196616 | tf_op jit(solution)/shard_map/ppermute | solution.py:352

commit v2 on v1

--- a/solution.py
+++ b/solution.py
@@ -44,19 +44,16 @@
     return pltpu.with_memory_space_constraint(values, pltpu.MemorySpace.HBM)
 
 
-def cut_pieces(place, keys, values, group, question=()):
+def cut_pieces(place, keys, values, group):
     token_count = keys.shape[0]
 
     def kernel(place_ref, keys_ref, values_ref, *refs):
-        question_refs, refs = refs[: len(question)], refs[len(question) :]
-        pieces, cuts, sems = refs[:group], refs[group:-1], refs[-1]
+        pieces, sems = refs[:-1], refs[-1]
         pairs = []
         for step, piece in enumerate(pieces):
             cut = columns(place_ref[0] ^ step, HEAD_SIZE)
             for half, source in enumerate((keys_ref, values_ref)):
                 pairs.append((source.at[:, cut], piece.at[pl.ds(half * token_count, token_count)]))
-        for source, target in zip(question_refs, cuts):
-            pairs.append((source.at[:, columns(place_ref[0], target.shape[1])], target))
         copies = [
             pltpu.make_async_copy(source, target, sems.at[i])
             for i, (source, target) in enumerate(pairs)
@@ -66,19 +63,16 @@
         for copy in copies:
             copy.wait()
 
-    shapes = [jax.ShapeDtypeStruct((2 * token_count, HEAD_SIZE), keys.dtype)] * group + [
-        jax.ShapeDtypeStruct((array.shape[0], array.shape[1] // group), array.dtype)
-        for array in question
-    ]
+    shape = jax.ShapeDtypeStruct((2 * token_count, HEAD_SIZE), keys.dtype)
     return pl.pallas_call(
         kernel,
-        out_shape=shapes,
-        in_specs=[SMEM] + [ANY] * (2 + len(question)),
-        out_specs=[ANY] * len(shapes),
-        scratch_shapes=[pltpu.SemaphoreType.DMA((len(shapes) + group,))],
+        out_shape=[shape] * group,
+        in_specs=[SMEM, ANY, ANY],
+        out_specs=[ANY] * group,
+        scratch_shapes=[pltpu.SemaphoreType.DMA((2 * group,))],
         compiler_params=PARAMS,
         name="cut_pieces",
-    )(place, in_hbm(keys), in_hbm(values), *map(in_hbm, question))
+    )(place, in_hbm(keys), in_hbm(values))
 
 
 def query_copies(place, query_ref, steps, targets, sems):
@@ -95,23 +89,35 @@
     return [jax.ShapeDtypeStruct(shape, query.dtype)] * len(steps)
 
 
-def bring_queries(place, query, group, steps, piece):
+def bring_queries(place, query, group, steps, question, piece):
+    count = len(steps)
+
     def kernel(place_ref, query_ref, piece_ref, *refs):
-        copies = query_copies(place_ref[0], query_ref, steps, refs[:-1], refs[-1])
+        question_refs, refs = refs[: len(question)], refs[len(question) :]
+        targets, sems = refs[:-1], refs[-1]
+        copies = query_copies(place_ref[0], query_ref, steps, targets[:count], sems)
+        for at, (source, target) in enumerate(zip(question_refs, targets[count:])):
+            cut = columns(place_ref[0], target.shape[1])
+            copies.append(pltpu.make_async_copy(source.at[:, cut], target, sems.at[count + at]))
         for copy in copies:
             copy.start()
         for copy in copies:
             copy.wait()
 
+    shapes = query_shapes(query, group, steps)
+    for array in question:
+        shapes.append(
+            jax.ShapeDtypeStruct((array.shape[0], array.shape[1] // group), array.dtype)
+        )
     return pl.pallas_call(
         kernel,
-        out_shape=query_shapes(query, group, steps),
-        in_specs=[SMEM, ANY, ANY],
-        out_specs=[ANY] * len(steps),
-        scratch_shapes=[pltpu.SemaphoreType.DMA((len(steps),))],
+        out_shape=shapes,
+        in_specs=[SMEM, ANY, ANY] + [ANY] * len(question),
+        out_specs=[ANY] * len(shapes),
+        scratch_shapes=[pltpu.SemaphoreType.DMA((len(shapes),))],
         compiler_params=PARAMS,
         name="bring_queries",
-    )(place, in_hbm(query), piece)
+    )(place, in_hbm(query), piece, *map(in_hbm, question))
 
 
 def question_parts(place, query, own_keys, own_values, pieces, ring):
@@ -199,18 +205,20 @@
     )(*parts)
 
 
-def project(blocks, chunks, weight, row_count, unit_heads, splits, own_split):
+def project(place, chunks, weight, row_count, unit_heads, ring, splits):
     depth, width = unit_heads * HEAD_SIZE, weight.shape[1]
     arrays, spots = [], []
-    for array, start in chunks:
+    for group_step, ring_step, array, start in chunks:
         if not any(array is other for other in arrays):
             arrays.append(array)
-        spots.append((next(i for i, other in enumerate(arrays) if other is array), start))
-
-    def kernel(blocks_ref, split_ref, weight_ref, *refs):
+        which = next(i for i, other in enumerate(arrays) if other is array)
+        spots.append((group_step, ring_step, which, start))
+
+    def kernel(place_ref, weight_ref, *refs):
         array_refs, outs, total_ref = refs[: len(arrays)], refs[len(arrays) : -1], refs[-1]
         total = None
-        for at, (which, start) in enumerate(spots):
+        for group_step, ring_step, which, start in spots:
+            unit = (place_ref[0] ^ group_step) * ring + (place_ref[1] ^ ring_step)
             rows = jnp.concatenate(
                 [
                     array_refs[which][start + i * row_count : start + (i + 1) * row_count]
@@ -218,13 +226,13 @@
                 ],
                 axis=1,
             )
-            block = weight_ref[pl.ds(pl.multiple_of(blocks_ref[at] * depth, depth), depth)]
+            block = weight_ref[pl.ds(pl.multiple_of(unit * depth, depth), depth)]
             term = dot_nn(rows, block)
             total = term if total is None else total + term
         total_ref[...] = total
         span = row_count // splits
         for step, out in enumerate(outs):
-            start = pl.multiple_of((split_ref[0] ^ step) * span, span)
+            start = pl.multiple_of((place_ref[2] ^ step) * span, span)
             out[...] = total_ref[pl.ds(start, span)].astype(out.dtype)
 
     return pl.pallas_call(
@@ -235,12 +243,12 @@
             )
             for step in range(splits)
         ],
-        in_specs=[SMEM, SMEM, VMEM] + [VMEM] * len(arrays),
+        in_specs=[SMEM, VMEM] + [VMEM] * len(arrays),
         out_specs=[VMEM] * splits,
         scratch_shapes=[pltpu.VMEM((row_count, width), jnp.float32)],
         compiler_params=PARAMS,
         name="project",
-    )(blocks, own_split, weight, *arrays)
+    )(place, weight, *arrays)
 
 
 def document_heads(place, query, group, steps, own, anchors, near, ahead, written, weight):
@@ -279,7 +287,7 @@
             for copy in later:
                 copy.start()
         cuts = [columns(member ^ step, step_columns) for step in steps]
-        after_anchor = place_ref[1] > 0
+        after_anchor = place_ref[0] + place_ref[1] > 0
         visible = lax.broadcasted_iota(jnp.int32, (token_count, token_count), 0) >= (
             lax.broadcasted_iota(jnp.int32, (token_count, token_count), 1)
         )
@@ -406,7 +414,7 @@
     head_total = question_query.shape[1] // HEAD_SIZE
     position = lax.axis_index("ctx")
     member, turn = position % group, position // group
-    place = joined(member, turn)
+    place = joined(member, turn, lax.axis_index("head"))
 
     def in_group(values, step):
         return swapped(values, "ctx", ctx_size, step)
@@ -416,16 +424,16 @@
 
     whole_units = head_total % ctx_size == 0
     question = (question_query, prompt_keys, prompt_values) if whole_units else ()
-    cuts = cut_pieces(place, document_keys, document_values, group, question)
-    pieces, question = cuts[:group], cuts[group:]
-    own_pieces = pieces
+    own_pieces = cut_pieces(place, document_keys, document_values, group)
+    pieces = own_pieces
     pieces = [pieces[0]] + [in_group(pieces[step], step) for step in range(1, group)]
 
     half = max(1, group // 2)
     near = ()
     if whole_units:
-        near = bring_queries(place, document_query, group, range(half), own_pieces[0])
+        near = bring_queries(place, document_query, group, range(half), question, own_pieces[0])
         pieces, near = lax.optimization_barrier((pieces, near))
+        near, question = near[:half], near[half:]
 
     anchor = lax.select_n(member, *pieces) if group > 1 else pieces[0]
 
@@ -438,8 +446,6 @@
         arrived = lax.ppermute(anchor, "ctx", pairs)
         return jnp.where(turn % (2 * reach) == reach, arrived, anchor)
 
-    spot = joined(member, position)
-
     reach = ring // 2
     if not whole_units:
         while reach:
@@ -447,7 +453,7 @@
             reach //= 2
         anchors = [anchor] + [in_group(anchor, step) for step in range(1, group)]
         doc_attention = document_heads(
-            spot, document_query, group, range(group), own_pieces, anchors, (), (), None, None
+            place, document_query, group, range(group), own_pieces, anchors, (), (), None, None
         )[0]
         return doc_attention, question_by_reduction(
             question_query, document_keys, document_values, prompt_keys, prompt_values, out_weight
@@ -465,24 +471,24 @@
         anchor = sent_on(anchor, reach)
     shards = [attention] + [in_ring(attention, step) for step in range(1, ring)]
 
-    chunks = [((0, step), shards[step], 0) for step in range(ring)]
+    chunks = [(0, step, shards[step], 0) for step in range(ring)]
     both = jnp.concatenate([anchor, attention], axis=0)
     passed = jnp.concatenate(shards[1:], axis=0)
     beside = [in_group(both, step) for step in range(1, group)]
     far = [in_group(passed, step) for step in range(1, group)]
     anchors = [anchor] + beside
     for member_step in range(1, group):
-        chunks.append(((member_step, 0), beside[member_step - 1], anchor.shape[0]))
+        chunks.append((member_step, 0, beside[member_step - 1], anchor.shape[0]))
         for step in range(1, ring):
             chunks.append(
-                ((member_step, step), far[member_step - 1], (step - 1) * attention.shape[0])
+                (member_step, step, far[member_step - 1], (step - 1) * attention.shape[0])
             )
 
     doc_attention, calls = None, [range(half), range(half, group)][: 2 if group > 1 else 1]
     for steps in calls:
         last = steps[-1] == group - 1
         doc_attention, *brought = document_heads(
-            spot,
+            place,
             document_query,
             group,
             steps,
@@ -495,18 +501,7 @@
         )
         near = brought
     (near_weight,) = brought
-    blocks = [
-        (member ^ member_step) * ring + (turn ^ step) for (member_step, step), _, _ in chunks
-    ]
-    shares = project(
-        joined(*blocks),
-        [(array, start) for _, array, start in chunks],
-        near_weight,
-        row_count,
-        unit_heads,
-        head_size,
-        joined(lax.axis_index("head")),
-    )
+    shares = project(place, chunks, near_weight, row_count, unit_heads, ring, head_size)
     question_out = shares[0]
     for step in range(1, head_size):
         question_out = question_out + swapped(shares[step], "head", head_size, step).astype(

time: 57 us -> 56.8 us (level)
  no operation moved by 1% of the time
where the time goes in v2:
time: 56.8 us; the launch traced here: 56.2 us
  starting transfers between devices  28.7 us (51%)
  Pallas kernels  16.6 us (29%)
  waiting for transfers between devices  9.25 us (16%)
  between operations  0.87 us (2%)
  other arithmetic  0.79 us (1%)
    ppermute x16, starting transfers between devices, swapped(): lax.ppermute(values, axis, [(place, place ^ step) for place in range(size)])  22 us
    ppermute x16, waiting for transfers between devices, swapped(): lax.ppermute(values, axis, [(place, place ^ step) for place in range(size)])  9.24 us
    pallas_call x2, Pallas kernels, document_heads(): pl.pallas_call(kernel, out_shape=out_shape, in_specs=[SMEM, ANY] + [VMEM]...  8.83 us
    ppermute x2, starting transfers between devices, sent_on(): arrived = lax.ppermute(anchor, 'ctx', pairs)  6.62 us
    pallas_call x1, Pallas kernels, question_parts(): pl.pallas_call(kernel, out_shape=[jax.ShapeDtypeStruct(out_shape, jnp.bfl...  2.42 us
    pallas_call x1, Pallas kernels, bring_queries(): pl.pallas_call(kernel, out_shape=shapes, in_specs=[SMEM, ANY, ANY] + [ANY...  1.86 us
    pallas_call x1, Pallas kernels, cut_pieces(): pl.pallas_call(kernel, out_shape=[shape] * group, in_specs=[SMEM, ANY, AN...  1.69 us
    pallas_call x1, Pallas kernels, project(): pl.pallas_call(kernel, out_shape=[jax.ShapeDtypeStruct((row_count // spli...  1.28 us
  transfers between devices with their start and end apart: 18, of which 8 were waited for; matrix products, arithmetic and copies ran while one was open for 0% of the time, Pallas kernels for 23%

profile of v2, /device:TPU:1, one launch (start us, length us, event | category | flops | bytes accessed | tf_op | source)
XLA Modules:
  0.0 56.2 jit_solution(14792763846698448766)
XLA Ops:
  0.7 0.1 pad_add_fusion.place_ref
  0.7 1.7 %cut_pieces.1 = (bf16[512,128]{1,0:T(8,128)(2,1)S(1)}, bf16[512,128]{1,0:T(8,128)(2,1)S(1)}, bf16[512,128]{1,0:T(8,128)(2,1)S(1)}, bf16[512,128]{1,0:T(8,128)(2,1)S(1)}) custom-call(s32[3]{0:T(128)S(1)} %pad_add_fusion.place_ref, bf16[256,512]{1,0:T(8,128)(2,1)} %keys_ref.1, bf16[256,512]{1,0:T(8,128)(2,1)} %values_ref.1), custom_call_target="tpu_custom_call" | custom-call | tf_op jit(solution)/shard_map/cut_pieces/pallas_call | solution.py:67
  2.4 2.1 %collective-permute-start = (bf16[512,128]{1,0:T(8,128)(2,1)S(1)}, bf16[512,128]{1,0:T(8,128)(2,1)S(1)}, u32[]{:S(2)}, u32[]{:S(2)}) collective-permute-start(bf16[512,128]{1,0:T(8,128)(2,1)S(1)} %get-tuple-element.39.refs_1_), channel_id=1, source_target_pairs={{0,2},{2,0},{4,6},{6,4},{8,10},{10,8},{12,14},{14,12},{16,18},{18,... | collective-permute-start | bytes 393224 | tf_op jit(solution)/shard_map/ppermute | solution.py:360
  4.5 1.2 %collective-permute-start.1 = (bf16[512,128]{1,0:T(8,128)(2,1)S(1)}, bf16[512,128]{1,0:T(8,128)(2,1)S(1)}, u32[]{:S(2)}, u32[]{:S(2)}) collective-permute-start(bf16[512,128]{1,0:T(8,128)(2,1)S(1)} %get-tuple-element.36.refs_0_), channel_id=1, source_target_pairs={{0,4},{2,6},{4,0},{6,2},{8,12},{10,14},{12,8},{14,10},{16,20},{18,... | collective-permute-start | bytes 393224 | tf_op jit(solution)/shard_map/ppermute | solution.py:360
  5.8 1.9 %bring_queries.1 = (bf16[256,1024]{1,0:T(8,128)(2,1)S(1)}, bf16[256,1024]{1,0:T(8,128)(2,1)S(1)}, bf16[128,1024]{1,0:T(8,128)(2,1)S(1)}, bf16[128,128]{1,0:T(8,128)(2,1)S(1)}, bf16[128,128]{1,0:T(8,128)(2,1)S(1)}) custom-call(s32[3]{0:T(128)S(1)} %pad_add_fusion.place_ref, bf16[256,4096]{1,0:T(8,128)(2,1)} %query_ref.5, ...), custom_call_target="tpu_custom_call" | custom-call | tf_op jit(solution)/shard_map/bring_queries/pallas_call | solution.py:112
  7.7 0.1 collective-permute-done.refs_1_
  7.8 0.9 %collective-permute-done.1.refs_2_ = bf16[512,128]{1,0:T(8,128)(2,1)S(1)} collective-permute-done((bf16[512,128]{1,0:T(8,128)(2,1)S(1)}, bf16[512,128]{1,0:T(8,128)(2,1)S(1)}, u32[]{:S(2)}, u32[]{:S(2)}) %collective-permute-start.1) | collective-permute-done | bytes 131104 | tf_op jit(solution)/shard_map/ppermute | solution.py:360
  8.6 2.7 %collective-permute-done.2.refs_3_ = bf16[512,128]{1,0:T(8,128)(2,1)S(1)} collective-permute-done((bf16[512,128]{1,0:T(8,128)(2,1)S(1)}, bf16[512,128]{1,0:T(8,128)(2,1)S(1)}, u32[]{:S(2)}, u32[]{:S(2)}) %collective-permute-start.2) | collective-permute-done | bytes 131104 | tf_op jit(solution)/shard_map/ppermute | solution.py:360
  11.3 4.2 %collective-permute-start.6 = (bf16[512,128]{1,0:T(8,128)(2,1)S(1)}, bf16[512,128]{1,0:T(8,128)(2,1)S(1)}, u32[]{:S(2)}, u32[]{:S(2)}) collective-permute-start(bf16[512,128]{1,0:T(8,128)(2,1)S(1)} %select_select_fusion), channel_id=1, source_target_pairs={{0,16},{2,18},{4,20},{6,22},{1,17},{3,19},{5,21},{7,23}} | collective-permute-start | bytes 393224 | tf_op jit(solution)/shard_map/ppermute | solution.py:446
  15.6 2.4 %question_parts.1 = (bf16[272,128]{1,0:T(8,128)(2,1)S(1)}, bf16[272,128]{1,0:T(8,128)(2,1)S(1)}, bf16[272,128]{1,0:T(8,128)(2,1)S(1)}, bf16[272,128]{1,0:T(8,128)(2,1)S(1)}) custom-call(s32[3]{0:T(128)S(1)} %pad_add_fusion.place_ref, bf16[128,1024]{1,0:T(8,128)(2,1)S(1)} %get-tuple-element.45.query_ref, bf16[128,128]{1,0:T(8,128)(2,1)S(1)} %get-tuple-element.46.own_keys_ref, ...), custom_call_target="tpu_custom_call" | custom-call | tf_op jit(solution)/shard_map/question_parts/pallas_call | solution.py:169
  18.0 0.1 collective-permute-start.3
  18.2 3.5 %collective-permute-start.5 = (bf16[272,128]{1,0:T(8,128)(2,1)S(1)}, bf16[272,128]{1,0:T(8,128)(2,1)S(1)}, u32[]{:S(2)}, u32[]{:S(2)}) collective-permute-start(bf16[272,128]{1,0:T(8,128)(2,1)S(1)} %get-tuple-element.55), channel_id=1, source_target_pairs={{0,24},{2,26},{4,28},{6,30},{8,16},{10,18},{12,20},{14,22},{16,8},... | collective-permute-start | bytes 208904 | tf_op jit(solution)/shard_map/ppermute | solution.py:360
  21.7 0.6 collective-permute-done.4.refs_2_
  22.2 2.2 %collective-permute-done.5.refs_3_ = bf16[272,128]{1,0:T(8,128)(2,1)S(1)} collective-permute-done((bf16[272,128]{1,0:T(8,128)(2,1)S(1)}, bf16[272,128]{1,0:T(8,128)(2,1)S(1)}, u32[]{:S(2)}, u32[]{:S(2)}) %collective-permute-start.5) | collective-permute-done | bytes 69664 | tf_op jit(solution)/shard_map/ppermute | solution.py:360
  24.4 0.5 merge_parts.1.refs_0_
  24.9 1.0 %collective-permute-start.11 = (bf16[256,128]{1,0:T(8,128)(2,1)S(1)}, bf16[256,128]{1,0:T(8,128)(2,1)S(1)}, u32[]{:S(2)}, u32[]{:S(2)}) collective-permute-start(bf16[256,128]{1,0:T(8,128)(2,1)S(1)} %merge_parts.1.refs_0_), channel_id=1, source_target_pairs={{0,8},{2,10},{4,12},{6,14},{8,0},{10,2},{12,4},{14,6},{16,24},{18,... | collective-permute-start | bytes 196616 | tf_op jit(solution)/shard_map/ppermute | solution.py:360
  25.9 2.4 %collective-permute-start.7 = (bf16[512,128]{1,0:T(8,128)(2,1)S(1)}, bf16[512,128]{1,0:T(8,128)(2,1)S(1)}, u32[]{:S(2)}, u32[]{:S(2)}) collective-permute-start(bf16[512,128]{1,0:T(8,128)(2,1)S(1)} %broadcast_select_fusion), channel_id=1, source_target_pairs={{0,8},{2,10},{4,12},{6,14},{16,24},{18,26},{20,28},{22,30},{1,9},{... | collective-permute-start | bytes 393224 | tf_op jit(solution)/shard_map/ppermute | solution.py:446
  28.4 2.8 %collective-permute-start.12 = (bf16[256,128]{1,0:T(8,128)(2,1)S(1)}, bf16[256,128]{1,0:T(8,128)(2,1)S(1)}, u32[]{:S(2)}, u32[]{:S(2)}) collective-permute-start(bf16[256,128]{1,0:T(8,128)(2,1)S(1)} %merge_parts.1.refs_0_), channel_id=1, source_target_pairs={{0,16},{2,18},{4,20},{6,22},{8,24},{10,26},{12,28},{14,30},{16,0},... | collective-permute-start | bytes 196616 | tf_op jit(solution)/shard_map/ppermute | solution.py:360
  31.2 1.0 %collective-permute-start.10 = (bf16[768,128]{1,0:T(8,128)(2,1)S(1)}, bf16[768,128]{1,0:T(8,128)(2,1)S(1)}, u32[]{:S(2)}, u32[]{:S(2)}) collective-permute-start(bf16[768,128]{1,0:T(8,128)(2,1)S(1)} %pad_maximum_fusion), channel_id=1, source_target_pairs={{0,2},{2,0},{4,6},{6,4},{8,10},{10,8},{12,14},{14,12},{16,18},{18,... | collective-permute-start | bytes 589832 | tf_op jit(solution)/shard_map/ppermute | solution.py:360
  32.3 0.5 collective-permute-done.12.refs_2_
  32.8 0.5 collective-permute-start.8
  33.3 1.7 %collective-permute-start.9 = (bf16[768,128]{1,0:T(8,128)(2,1)S(1)}, bf16[768,128]{1,0:T(8,128)(2,1)S(1)}, u32[]{:S(2)}, u32[]{:S(2)}) collective-permute-start(bf16[768,128]{1,0:T(8,128)(2,1)S(1)} %pad_maximum_fusion), channel_id=1, source_target_pairs={{0,6},{2,4},{4,2},{6,0},{8,14},{10,12},{12,10},{14,8},{16,22},{18,... | collective-permute-start | bytes 589832 | tf_op jit(solution)/shard_map/ppermute | solution.py:360
  35.1 1.4 %collective-permute-done.13.refs_3_ = bf16[256,128]{1,0:T(8,128)(2,1)S(1)} collective-permute-done((bf16[256,128]{1,0:T(8,128)(2,1)S(1)}, bf16[256,128]{1,0:T(8,128)(2,1)S(1)}, u32[]{:S(2)}, u32[]{:S(2)}) %collective-permute-start.13) | collective-permute-done | bytes 65568 | tf_op jit(solution)/shard_map/ppermute | solution.py:360
  36.5 1.0 %collective-permute-start.14 = (bf16[768,128]{1,0:T(8,128)(2,1)S(1)}, bf16[768,128]{1,0:T(8,128)(2,1)S(1)}, u32[]{:S(2)}, u32[]{:S(2)}) collective-permute-start(bf16[768,128]{1,0:T(8,128)(2,1)S(1)} %constant_dynamic-update-slice_fusion), channel_id=1, source_target_pairs={{0,2},{2,0},{4,6},{6,4},{8,10},{10,8},{12,14},{14,12},{16,18},{18,... | collective-permute-start | bytes 589832 | tf_op jit(solution)/shard_map/ppermute | solution.py:360
  37.5 0.5 collective-permute-start.15
  38.0 1.2 %collective-permute-start.16 = (bf16[768,128]{1,0:T(8,128)(2,1)S(1)}, bf16[768,128]{1,0:T(8,128)(2,1)S(1)}, u32[]{:S(2)}, u32[]{:S(2)}) collective-permute-start(bf16[768,128]{1,0:T(8,128)(2,1)S(1)} %constant_dynamic-update-slice_fusion), channel_id=1, source_target_pairs={{0,6},{2,4},{4,2},{6,0},{8,14},{10,12},{12,10},{14,8},{16,22},{18,... | collective-permute-start | bytes 589832 | tf_op jit(solution)/shard_map/ppermute | solution.py:360
  39.2 4.6 %document_heads.2 = (bf16[256,4096]{1,0:T(8,128)(2,1)}, bf16[256,1024]{1,0:T(8,128)(2,1)S(1)}, bf16[256,1024]{1,0:T(8,128)(2,1)S(1)}) custom-call(s32[3]{0:T(128)S(1)} %pad_add_fusion.place_ref, bf16[256,4096]{1,0:T(8,128)(2,1)} %query_ref.5, bf16[512,128]{1,0:T(8,128)(2,1)S(1)} %get-tuple-element.48.piece_ref.refs_0_, ...), custom_call_target="tpu_custom_call" | custom-call | tf_op jit(solution)/shard_map/document_heads/pallas_call | solution.py:343
  43.8 4.2 %document_heads.3 = (bf16[256,4096]{1,0:T(8,128)(2,1)}, bf16[4096,512]{1,0:T(8,128)(2,1)S(1)}) custom-call(s32[3]{0:T(128)S(1)} %pad_add_fusion.place_ref, bf16[256,4096]{1,0:T(8,128)(2,1)} %query_ref.5, bf16[512,128]{1,0:T(8,128)(2,1)S(1)} %get-tuple-element.36.refs_0_, ...), custom_call_target="tpu_custom_call", output_to_operand_aliasing={{0}: (8, {})} | custom-call | tf_op jit(solution)/shard_map/document_heads/pallas_call | solution.py:343
  48.1 1.3 %project.1 = (f32[64,512]{1,0:T(8,128)S(1)}, bf16[64,512]{1,0:T(8,128)(2,1)S(1)}) custom-call(s32[3]{0:T(128)S(1)} %pad_add_fusion.place_ref, bf16[4096,512]{1,0:T(8,128)(2,1)S(1)} %get-tuple-element.67.weight_ref, bf16[256,128]{1,0:T(8,128)(2,1)S(1)} %merge_parts.1.refs_0_, bf16[256,128]{1,0:T(8,128)(2,1)S(1)} %collective-permute-done.11.refs_1_, ...), custom_call_target="tpu_custom_call" | custom-call | tf_op jit(solution)/shard_map/project/pallas_call | solution.py:238
  49.4 5.3 %collective-permute-start.17 = (bf16[64,512]{1,0:T(8,128)(2,1)S(1)}, bf16[64,512]{1,0:T(8,128)(2,1)S(1)}, u32[]{:S(2)}, u32[]{:S(2)}) collective-permute-start(bf16[64,512]{1,0:T(8,128)(2,1)S(1)} %get-tuple-element.69), channel_id=1, source_target_pairs={{0,1},{1,0},{2,3},{3,2},{4,5},{5,4},{6,7},{7,6},{8,9},{9,8},{10,11... | collective-permute-start | bytes 196616 | tf_op jit(solution)/shard_map/ppermute | solution.py:360
  54.6 0.9 %collective-permute-done.17 = bf16[64,512]{1,0:T(8,128)(2,1)S(1)} collective-permute-done((bf16[64,512]{1,0:T(8,128)(2,1)S(1)}, bf16[64,512]{1,0:T(8,128)(2,1)S(1)}, u32[]{:S(2)}, u32[]{:S(2)}) %collective-permute-start.17) | collective-permute-done | bytes 65568 | tf_op jit(solution)/shard_map/ppermute | solution.py:360
  55.5 0.6 %add_convert_fusion = bf16[64,512]{1,0:T(8,128)(2,1)} fusion(f32[64,512]{1,0:T(8,128)S(1)} %get-tuple-element.68, bf16[64,512]{1,0:T(8,128)(2,1)S(1)} %collective-permute-done.17), kind=kLoop, calls=%fused_computation.1 | loop fusion | flops 98304 | bytes 262144 | tf_op jit(solution)/shard_map/convert_element_type | solution.py:510
  (20 shorter events, 0.2 us)
Async XLA Ops:
  2.4 5.3 %collective-permute-start = (bf16[512,128]{1,0:T(8,128)(2,1)S(1)}, bf16[512,128]{1,0:T(8,128)(2,1)S(1)}, u32[]{:S(2)}, u32[]{:S(2)}) collective-permute-start(bf16[512,128]{1,0:T(8,128)(2,1)S(1)} %get-tuple-element.39.refs_1_), channel_id=1, source_target_pairs={{0,2},{2,0},{4,6},{6,4},{8,10},{10,8},{12,14},{14,12},{16,18},{18,... | collective-permute-start | bytes 393224 | tf_op jit(solution)/shard_map/ppermute | solution.py:360
  4.5 4.1 %collective-permute-start.1 = (bf16[512,128]{1,0:T(8,128)(2,1)S(1)}, bf16[512,128]{1,0:T(8,128)(2,1)S(1)}, u32[]{:S(2)}, u32[]{:S(2)}) collective-permute-start(bf16[512,128]{1,0:T(8,128)(2,1)S(1)} %get-tuple-element.36.refs_0_), channel_id=1, source_target_pairs={{0,4},{2,6},{4,0},{6,2},{8,12},{10,14},{12,8},{14,10},{16,20},{18,... | collective-permute-start | bytes 393224 | tf_op jit(solution)/shard_map/ppermute | solution.py:360
  5.8 5.5 %collective-permute-start.2 = (bf16[512,128]{1,0:T(8,128)(2,1)S(1)}, bf16[512,128]{1,0:T(8,128)(2,1)S(1)}, u32[]{:S(2)}, u32[]{:S(2)}) collective-permute-start(bf16[512,128]{1,0:T(8,128)(2,1)S(1)} %get-tuple-element.37.refs_1_), channel_id=1, source_target_pairs={{0,6},{2,4},{4,2},{6,0},{8,14},{10,12},{12,10},{14,8},{16,22},{18,... | collective-permute-start | bytes 393224 | tf_op jit(solution)/shard_map/ppermute | solution.py:360
  11.3 10.3 %collective-permute-start.6 = (bf16[512,128]{1,0:T(8,128)(2,1)S(1)}, bf16[512,128]{1,0:T(8,128)(2,1)S(1)}, u32[]{:S(2)}, u32[]{:S(2)}) collective-permute-start(bf16[512,128]{1,0:T(8,128)(2,1)S(1)} %select_select_fusion), channel_id=1, source_target_pairs={{0,16},{2,18},{4,20},{6,22},{1,17},{3,19},{5,21},{7,23}} | collective-permute-start | bytes 393224 | tf_op jit(solution)/shard_map/ppermute | solution.py:446
  18.0 3.6 %collective-permute-start.3 = (bf16[272,128]{1,0:T(8,128)(2,1)S(1)}, bf16[272,128]{1,0:T(8,128)(2,1)S(1)}, u32[]{:S(2)}, u32[]{:S(2)}) collective-permute-start(bf16[272,128]{1,0:T(8,128)(2,1)S(1)} %get-tuple-element.53), channel_id=1, source_target_pairs={{0,8},{2,10},{4,12},{6,14},{8,0},{10,2},{12,4},{14,6},{16,24},{18,... | collective-permute-start | bytes 208904 | tf_op jit(solution)/shard_map/ppermute | solution.py:360
  18.1 4.1 %collective-permute-start.4 = (bf16[272,128]{1,0:T(8,128)(2,1)S(1)}, bf16[272,128]{1,0:T(8,128)(2,1)S(1)}, u32[]{:S(2)}, u32[]{:S(2)}) collective-permute-start(bf16[272,128]{1,0:T(8,128)(2,1)S(1)} %get-tuple-element.54), channel_id=1, source_target_pairs={{0,16},{2,18},{4,20},{6,22},{8,24},{10,26},{12,28},{14,30},{16,0},... | collective-permute-start | bytes 208904 | tf_op jit(solution)/shard_map/ppermute | solution.py:360
  18.2 6.2 %collective-permute-start.5 = (bf16[272,128]{1,0:T(8,128)(2,1)S(1)}, bf16[272,128]{1,0:T(8,128)(2,1)S(1)}, u32[]{:S(2)}, u32[]{:S(2)}) collective-permute-start(bf16[272,128]{1,0:T(8,128)(2,1)S(1)} %get-tuple-element.55), channel_id=1, source_target_pairs={{0,24},{2,26},{4,28},{6,30},{8,16},{10,18},{12,20},{14,22},{16,8},... | collective-permute-start | bytes 208904 | tf_op jit(solution)/shard_map/ppermute | solution.py:360
  24.9 6.3 %collective-permute-start.11 = (bf16[256,128]{1,0:T(8,128)(2,1)S(1)}, bf16[256,128]{1,0:T(8,128)(2,1)S(1)}, u32[]{:S(2)}, u32[]{:S(2)}) collective-permute-start(bf16[256,128]{1,0:T(8,128)(2,1)S(1)} %merge_parts.1.refs_0_), channel_id=1, source_target_pairs={{0,8},{2,10},{4,12},{6,14},{8,0},{10,2},{12,4},{14,6},{16,24},{18,... | collective-permute-start | bytes 196616 | tf_op jit(solution)/shard_map/ppermute | solution.py:360
  25.9 5.2 %collective-permute-start.7 = (bf16[512,128]{1,0:T(8,128)(2,1)S(1)}, bf16[512,128]{1,0:T(8,128)(2,1)S(1)}, u32[]{:S(2)}, u32[]{:S(2)}) collective-permute-start(bf16[512,128]{1,0:T(8,128)(2,1)S(1)} %broadcast_select_fusion), channel_id=1, source_target_pairs={{0,8},{2,10},{4,12},{6,14},{16,24},{18,26},{20,28},{22,30},{1,9},{... | collective-permute-start | bytes 393224 | tf_op jit(solution)/shard_map/ppermute | solution.py:446
  28.4 4.4 %collective-permute-start.12 = (bf16[256,128]{1,0:T(8,128)(2,1)S(1)}, bf16[256,128]{1,0:T(8,128)(2,1)S(1)}, u32[]{:S(2)}, u32[]{:S(2)}) collective-permute-start(bf16[256,128]{1,0:T(8,128)(2,1)S(1)} %merge_parts.1.refs_0_), channel_id=1, source_target_pairs={{0,16},{2,18},{4,20},{6,22},{8,24},{10,26},{12,28},{14,30},{16,0},... | collective-permute-start | bytes 196616 | tf_op jit(solution)/shard_map/ppermute | solution.py:360
  31.2 5.3 %collective-permute-start.13 = (bf16[256,128]{1,0:T(8,128)(2,1)S(1)}, bf16[256,128]{1,0:T(8,128)(2,1)S(1)}, u32[]{:S(2)}, u32[]{:S(2)}) collective-permute-start(bf16[256,128]{1,0:T(8,128)(2,1)S(1)} %merge_parts.1.refs_0_), channel_id=1, source_target_pairs={{0,24},{2,26},{4,28},{6,30},{8,16},{10,18},{12,20},{14,22},{16,8},... | collective-permute-start | bytes 196616 | tf_op jit(solution)/shard_map/ppermute | solution.py:360
  31.2 6.8 %collective-permute-start.10 = (bf16[768,128]{1,0:T(8,128)(2,1)S(1)}, bf16[768,128]{1,0:T(8,128)(2,1)S(1)}, u32[]{:S(2)}, u32[]{:S(2)}) collective-permute-start(bf16[768,128]{1,0:T(8,128)(2,1)S(1)} %pad_maximum_fusion), channel_id=1, source_target_pairs={{0,2},{2,0},{4,6},{6,4},{8,10},{10,8},{12,14},{14,12},{16,18},{18,... | collective-permute-start | bytes 589832 | tf_op jit(solution)/shard_map/ppermute | solution.py:360
  32.8 10.9 %collective-permute-start.8 = (bf16[768,128]{1,0:T(8,128)(2,1)S(1)}, bf16[768,128]{1,0:T(8,128)(2,1)S(1)}, u32[]{:S(2)}, u32[]{:S(2)}) collective-permute-start(bf16[768,128]{1,0:T(8,128)(2,1)S(1)} %pad_maximum_fusion), channel_id=1, source_target_pairs={{0,4},{2,6},{4,0},{6,2},{8,12},{10,14},{12,8},{14,10},{16,20},{18,... | collective-permute-start | bytes 589832 | tf_op jit(solution)/shard_map/ppermute | solution.py:360
  33.3 10.5 %collective-permute-start.9 = (bf16[768,128]{1,0:T(8,128)(2,1)S(1)}, bf16[768,128]{1,0:T(8,128)(2,1)S(1)}, u32[]{:S(2)}, u32[]{:S(2)}) collective-permute-start(bf16[768,128]{1,0:T(8,128)(2,1)S(1)} %pad_maximum_fusion), channel_id=1, source_target_pairs={{0,6},{2,4},{4,2},{6,0},{8,14},{10,12},{12,10},{14,8},{16,22},{18,... | collective-permute-start | bytes 589832 | tf_op jit(solution)/shard_map/ppermute | solution.py:360
  36.5 11.6 %collective-permute-start.14 = (bf16[768,128]{1,0:T(8,128)(2,1)S(1)}, bf16[768,128]{1,0:T(8,128)(2,1)S(1)}, u32[]{:S(2)}, u32[]{:S(2)}) collective-permute-start(bf16[768,128]{1,0:T(8,128)(2,1)S(1)} %constant_dynamic-update-slice_fusion), channel_id=1, source_target_pairs={{0,2},{2,0},{4,6},{6,4},{8,10},{10,8},{12,14},{14,12},{16,18},{18,... | collective-permute-start | bytes 589832 | tf_op jit(solution)/shard_map/ppermute | solution.py:360
  37.5 10.6 %collective-permute-start.15 = (bf16[768,128]{1,0:T(8,128)(2,1)S(1)}, bf16[768,128]{1,0:T(8,128)(2,1)S(1)}, u32[]{:S(2)}, u32[]{:S(2)}) collective-permute-start(bf16[768,128]{1,0:T(8,128)(2,1)S(1)} %constant_dynamic-update-slice_fusion), channel_id=1, source_target_pairs={{0,4},{2,6},{4,0},{6,2},{8,12},{10,14},{12,8},{14,10},{16,20},{18,... | collective-permute-start | bytes 589832 | tf_op jit(solution)/shard_map/ppermute | solution.py:360
  38.0 10.1 %collective-permute-start.16 = (bf16[768,128]{1,0:T(8,128)(2,1)S(1)}, bf16[768,128]{1,0:T(8,128)(2,1)S(1)}, u32[]{:S(2)}, u32[]{:S(2)}) collective-permute-start(bf16[768,128]{1,0:T(8,128)(2,1)S(1)} %constant_dynamic-update-slice_fusion), channel_id=1, source_target_pairs={{0,6},{2,4},{4,2},{6,0},{8,14},{10,12},{12,10},{14,8},{16,22},{18,... | collective-permute-start | bytes 589832 | tf_op jit(solution)/shard_map/ppermute | solution.py:360
  49.4 6.2 %collective-permute-start.17 = (bf16[64,512]{1,0:T(8,128)(2,1)S(1)}, bf16[64,512]{1,0:T(8,128)(2,1)S(1)}, u32[]{:S(2)}, u32[]{:S(2)}) collective-permute-start(bf16[64,512]{1,0:T(8,128)(2,1)S(1)} %get-tuple-element.69), channel_id=1, source_target_pairs={{0,1},{1,0},{2,3},{3,2},{4,5},{5,4},{6,7},{7,6},{8,9},{9,8},{10,11... | collective-permute-start | bytes 196616 | tf_op jit(solution)/shard_map/ppermute | solution.py:360

commit v3 on v2

--- a/solution.py
+++ b/solution.py
@@ -301,22 +301,22 @@
                 for copy in later:
                     copy.start()
             pair = (anchor_refs[step], own_refs[step])
-            all_keys = jnp.concatenate([ref[:token_count] for ref in pair], axis=0)
-            all_values = with_ones(
-                jnp.concatenate([ref[token_count : 2 * token_count] for ref in pair], axis=0)
+            anchor_keys, own_keys = (ref[:token_count] for ref in pair)
+            anchor_values, own_values = (
+                with_ones(ref[token_count : 2 * token_count]) for ref in pair
             )
             for head in range(GROUP_WIDTH):
                 spot = slice(head * HEAD_SIZE, (head + 1) * HEAD_SIZE)
-                scores = dot_nt(near_refs[step][:, spot], all_keys)
-                anchor_scores = scores[:, :token_count]
-                own_scores = jnp.where(visible, scores[:, token_count:], NEG_INF)
+                queries = near_refs[step][:, spot]
+                anchor_scores = dot_nt(queries, anchor_keys)
+                own_scores = jnp.where(visible, dot_nt(queries, own_keys), NEG_INF)
                 own_top = own_scores.max(axis=1, keepdims=True)
                 anchor_top = anchor_scores.max(axis=1, keepdims=True)
                 top = jnp.where(after_anchor, jnp.maximum(own_top, anchor_top), own_top) * scale
                 anchor_shift = jnp.where(after_anchor, top, 1e30)
                 anchor_exp = jnp.exp2(anchor_scores * scale - anchor_shift).astype(jnp.bfloat16)
                 own_exp = jnp.exp2(own_scores * scale - top).astype(jnp.bfloat16)
-                mixture = dot_nn(jnp.concatenate([anchor_exp, own_exp], axis=1), all_values)
+                mixture = dot_nn(anchor_exp, anchor_values) + dot_nn(own_exp, own_values)
                 held[step, :, spot] = (mixture[:, :HEAD_SIZE] / mixture[:, HEAD_SIZE:]).astype(
                     held.dtype
                 )

time: 56.8 us -> 56.8 us (level)
  no operation moved by 1% of the time
where the time goes in v3:
time: 56.8 us; the launch traced here: 56.2 us
  starting transfers between devices  28.7 us (51%)
  Pallas kernels  16.6 us (29%)
  waiting for transfers between devices  9.25 us (16%)
  between operations  0.87 us (2%)
  other arithmetic  0.79 us (1%)
    ppermute x16, starting transfers between devices, swapped(): lax.ppermute(values, axis, [(place, place ^ step) for place in range(size)])  22 us
    ppermute x16, waiting for transfers between devices, swapped(): lax.ppermute(values, axis, [(place, place ^ step) for place in range(size)])  9.24 us
    pallas_call x2, Pallas kernels, document_heads(): pl.pallas_call(kernel, out_shape=out_shape, in_specs=[SMEM, ANY] + [VMEM]...  8.83 us
    ppermute x2, starting transfers between devices, sent_on(): arrived = lax.ppermute(anchor, 'ctx', pairs)  6.62 us
    pallas_call x1, Pallas kernels, question_parts(): pl.pallas_call(kernel, out_shape=[jax.ShapeDtypeStruct(out_shape, jnp.bfl...  2.42 us
    pallas_call x1, Pallas kernels, bring_queries(): pl.pallas_call(kernel, out_shape=shapes, in_specs=[SMEM, ANY, ANY] + [ANY...  1.86 us
    pallas_call x1, Pallas kernels, cut_pieces(): pl.pallas_call(kernel, out_shape=[shape] * group, in_specs=[SMEM, ANY, AN...  1.69 us
    pallas_call x1, Pallas kernels, project(): pl.pallas_call(kernel, out_shape=[jax.ShapeDtypeStruct((row_count // spli...  1.28 us
  transfers between devices with their start and end apart: 18, of which 8 were waited for; matrix products, arithmetic and copies ran while one was open for 0% of the time, Pallas kernels for 23%

profile of v3, /device:TPU:1, one launch (start us, length us, event | category | flops | bytes accessed | tf_op | source)
XLA Modules:
  0.0 56.2 jit_solution(3562078494180140360)
XLA Ops:
  0.7 0.1 pad_add_fusion.place_ref
  0.7 1.7 %cut_pieces.1 = (bf16[512,128]{1,0:T(8,128)(2,1)S(1)}, bf16[512,128]{1,0:T(8,128)(2,1)S(1)}, bf16[512,128]{1,0:T(8,128)(2,1)S(1)}, bf16[512,128]{1,0:T(8,128)(2,1)S(1)}) custom-call(s32[3]{0:T(128)S(1)} %pad_add_fusion.place_ref, bf16[256,512]{1,0:T(8,128)(2,1)} %keys_ref.1, bf16[256,512]{1,0:T(8,128)(2,1)} %values_ref.1), custom_call_target="tpu_custom_call" | custom-call | tf_op jit(solution)/shard_map/cut_pieces/pallas_call | solution.py:67
  2.4 2.1 %collective-permute-start = (bf16[512,128]{1,0:T(8,128)(2,1)S(1)}, bf16[512,128]{1,0:T(8,128)(2,1)S(1)}, u32[]{:S(2)}, u32[]{:S(2)}) collective-permute-start(bf16[512,128]{1,0:T(8,128)(2,1)S(1)} %get-tuple-element.39.refs_1_), channel_id=1, source_target_pairs={{0,2},{2,0},{4,6},{6,4},{8,10},{10,8},{12,14},{14,12},{16,18},{18,... | collective-permute-start | bytes 393224 | tf_op jit(solution)/shard_map/ppermute | solution.py:360
  4.5 1.2 %collective-permute-start.1 = (bf16[512,128]{1,0:T(8,128)(2,1)S(1)}, bf16[512,128]{1,0:T(8,128)(2,1)S(1)}, u32[]{:S(2)}, u32[]{:S(2)}) collective-permute-start(bf16[512,128]{1,0:T(8,128)(2,1)S(1)} %get-tuple-element.36.refs_0_), channel_id=1, source_target_pairs={{0,4},{2,6},{4,0},{6,2},{8,12},{10,14},{12,8},{14,10},{16,20},{18,... | collective-permute-start | bytes 393224 | tf_op jit(solution)/shard_map/ppermute | solution.py:360
  5.8 1.9 %bring_queries.1 = (bf16[256,1024]{1,0:T(8,128)(2,1)S(1)}, bf16[256,1024]{1,0:T(8,128)(2,1)S(1)}, bf16[128,1024]{1,0:T(8,128)(2,1)S(1)}, bf16[128,128]{1,0:T(8,128)(2,1)S(1)}, bf16[128,128]{1,0:T(8,128)(2,1)S(1)}) custom-call(s32[3]{0:T(128)S(1)} %pad_add_fusion.place_ref, bf16[256,4096]{1,0:T(8,128)(2,1)} %query_ref.5, ...), custom_call_target="tpu_custom_call" | custom-call | tf_op jit(solution)/shard_map/bring_queries/pallas_call | solution.py:112
  7.7 0.1 collective-permute-done.refs_1_
  7.8 0.9 %collective-permute-done.1.refs_2_ = bf16[512,128]{1,0:T(8,128)(2,1)S(1)} collective-permute-done((bf16[512,128]{1,0:T(8,128)(2,1)S(1)}, bf16[512,128]{1,0:T(8,128)(2,1)S(1)}, u32[]{:S(2)}, u32[]{:S(2)}) %collective-permute-start.1) | collective-permute-done | bytes 131104 | tf_op jit(solution)/shard_map/ppermute | solution.py:360
  8.6 2.7 %collective-permute-done.2.refs_3_ = bf16[512,128]{1,0:T(8,128)(2,1)S(1)} collective-permute-done((bf16[512,128]{1,0:T(8,128)(2,1)S(1)}, bf16[512,128]{1,0:T(8,128)(2,1)S(1)}, u32[]{:S(2)}, u32[]{:S(2)}) %collective-permute-start.2) | collective-permute-done | bytes 131104 | tf_op jit(solution)/shard_map/ppermute | solution.py:360
  11.3 4.2 %collective-permute-start.6 = (bf16[512,128]{1,0:T(8,128)(2,1)S(1)}, bf16[512,128]{1,0:T(8,128)(2,1)S(1)}, u32[]{:S(2)}, u32[]{:S(2)}) collective-permute-start(bf16[512,128]{1,0:T(8,128)(2,1)S(1)} %select_select_fusion), channel_id=1, source_target_pairs={{0,16},{2,18},{4,20},{6,22},{1,17},{3,19},{5,21},{7,23}} | collective-permute-start | bytes 393224 | tf_op jit(solution)/shard_map/ppermute | solution.py:446
  15.6 2.4 %question_parts.1 = (bf16[272,128]{1,0:T(8,128)(2,1)S(1)}, bf16[272,128]{1,0:T(8,128)(2,1)S(1)}, bf16[272,128]{1,0:T(8,128)(2,1)S(1)}, bf16[272,128]{1,0:T(8,128)(2,1)S(1)}) custom-call(s32[3]{0:T(128)S(1)} %pad_add_fusion.place_ref, bf16[128,1024]{1,0:T(8,128)(2,1)S(1)} %get-tuple-element.45.query_ref, bf16[128,128]{1,0:T(8,128)(2,1)S(1)} %get-tuple-element.46.own_keys_ref, ...), custom_call_target="tpu_custom_call" | custom-call | tf_op jit(solution)/shard_map/question_parts/pallas_call | solution.py:169
  18.0 0.1 collective-permute-start.3
  18.2 3.5 %collective-permute-start.5 = (bf16[272,128]{1,0:T(8,128)(2,1)S(1)}, bf16[272,128]{1,0:T(8,128)(2,1)S(1)}, u32[]{:S(2)}, u32[]{:S(2)}) collective-permute-start(bf16[272,128]{1,0:T(8,128)(2,1)S(1)} %get-tuple-element.55), channel_id=1, source_target_pairs={{0,24},{2,26},{4,28},{6,30},{8,16},{10,18},{12,20},{14,22},{16,8},... | collective-permute-start | bytes 208904 | tf_op jit(solution)/shard_map/ppermute | solution.py:360
  21.7 0.6 collective-permute-done.4.refs_2_
  22.2 2.2 %collective-permute-done.5.refs_3_ = bf16[272,128]{1,0:T(8,128)(2,1)S(1)} collective-permute-done((bf16[272,128]{1,0:T(8,128)(2,1)S(1)}, bf16[272,128]{1,0:T(8,128)(2,1)S(1)}, u32[]{:S(2)}, u32[]{:S(2)}) %collective-permute-start.5) | collective-permute-done | bytes 69664 | tf_op jit(solution)/shard_map/ppermute | solution.py:360
  24.4 0.5 merge_parts.1.refs_0_
  24.9 1.0 %collective-permute-start.11 = (bf16[256,128]{1,0:T(8,128)(2,1)S(1)}, bf16[256,128]{1,0:T(8,128)(2,1)S(1)}, u32[]{:S(2)}, u32[]{:S(2)}) collective-permute-start(bf16[256,128]{1,0:T(8,128)(2,1)S(1)} %merge_parts.1.refs_0_), channel_id=1, source_target_pairs={{0,8},{2,10},{4,12},{6,14},{8,0},{10,2},{12,4},{14,6},{16,24},{18,... | collective-permute-start | bytes 196616 | tf_op jit(solution)/shard_map/ppermute | solution.py:360
  25.9 2.4 %collective-permute-start.7 = (bf16[512,128]{1,0:T(8,128)(2,1)S(1)}, bf16[512,128]{1,0:T(8,128)(2,1)S(1)}, u32[]{:S(2)}, u32[]{:S(2)}) collective-permute-start(bf16[512,128]{1,0:T(8,128)(2,1)S(1)} %broadcast_select_fusion), channel_id=1, source_target_pairs={{0,8},{2,10},{4,12},{6,14},{16,24},{18,26},{20,28},{22,30},{1,9},{... | collective-permute-start | bytes 393224 | tf_op jit(solution)/shard_map/ppermute | solution.py:446
  28.4 2.8 %collective-permute-start.12 = (bf16[256,128]{1,0:T(8,128)(2,1)S(1)}, bf16[256,128]{1,0:T(8,128)(2,1)S(1)}, u32[]{:S(2)}, u32[]{:S(2)}) collective-permute-start(bf16[256,128]{1,0:T(8,128)(2,1)S(1)} %merge_parts.1.refs_0_), channel_id=1, source_target_pairs={{0,16},{2,18},{4,20},{6,22},{8,24},{10,26},{12,28},{14,30},{16,0},... | collective-permute-start | bytes 196616 | tf_op jit(solution)/shard_map/ppermute | solution.py:360
  31.2 1.0 %collective-permute-start.10 = (bf16[768,128]{1,0:T(8,128)(2,1)S(1)}, bf16[768,128]{1,0:T(8,128)(2,1)S(1)}, u32[]{:S(2)}, u32[]{:S(2)}) collective-permute-start(bf16[768,128]{1,0:T(8,128)(2,1)S(1)} %pad_maximum_fusion), channel_id=1, source_target_pairs={{0,2},{2,0},{4,6},{6,4},{8,10},{10,8},{12,14},{14,12},{16,18},{18,... | collective-permute-start | bytes 589832 | tf_op jit(solution)/shard_map/ppermute | solution.py:360
  32.3 0.5 collective-permute-done.12.refs_2_
  32.8 0.5 collective-permute-start.8
  33.3 1.7 %collective-permute-start.9 = (bf16[768,128]{1,0:T(8,128)(2,1)S(1)}, bf16[768,128]{1,0:T(8,128)(2,1)S(1)}, u32[]{:S(2)}, u32[]{:S(2)}) collective-permute-start(bf16[768,128]{1,0:T(8,128)(2,1)S(1)} %pad_maximum_fusion), channel_id=1, source_target_pairs={{0,6},{2,4},{4,2},{6,0},{8,14},{10,12},{12,10},{14,8},{16,22},{18,... | collective-permute-start | bytes 589832 | tf_op jit(solution)/shard_map/ppermute | solution.py:360
  35.1 1.4 %collective-permute-done.13.refs_3_ = bf16[256,128]{1,0:T(8,128)(2,1)S(1)} collective-permute-done((bf16[256,128]{1,0:T(8,128)(2,1)S(1)}, bf16[256,128]{1,0:T(8,128)(2,1)S(1)}, u32[]{:S(2)}, u32[]{:S(2)}) %collective-permute-start.13) | collective-permute-done | bytes 65568 | tf_op jit(solution)/shard_map/ppermute | solution.py:360
  36.5 1.0 %collective-permute-start.14 = (bf16[768,128]{1,0:T(8,128)(2,1)S(1)}, bf16[768,128]{1,0:T(8,128)(2,1)S(1)}, u32[]{:S(2)}, u32[]{:S(2)}) collective-permute-start(bf16[768,128]{1,0:T(8,128)(2,1)S(1)} %constant_dynamic-update-slice_fusion), channel_id=1, source_target_pairs={{0,2},{2,0},{4,6},{6,4},{8,10},{10,8},{12,14},{14,12},{16,18},{18,... | collective-permute-start | bytes 589832 | tf_op jit(solution)/shard_map/ppermute | solution.py:360
  37.5 0.5 collective-permute-start.15
  38.0 1.2 %collective-permute-start.16 = (bf16[768,128]{1,0:T(8,128)(2,1)S(1)}, bf16[768,128]{1,0:T(8,128)(2,1)S(1)}, u32[]{:S(2)}, u32[]{:S(2)}) collective-permute-start(bf16[768,128]{1,0:T(8,128)(2,1)S(1)} %constant_dynamic-update-slice_fusion), channel_id=1, source_target_pairs={{0,6},{2,4},{4,2},{6,0},{8,14},{10,12},{12,10},{14,8},{16,22},{18,... | collective-permute-start | bytes 589832 | tf_op jit(solution)/shard_map/ppermute | solution.py:360
  39.2 4.6 %document_heads.2 = (bf16[256,4096]{1,0:T(8,128)(2,1)}, bf16[256,1024]{1,0:T(8,128)(2,1)S(1)}, bf16[256,1024]{1,0:T(8,128)(2,1)S(1)}) custom-call(s32[3]{0:T(128)S(1)} %pad_add_fusion.place_ref, bf16[256,4096]{1,0:T(8,128)(2,1)} %query_ref.5, bf16[512,128]{1,0:T(8,128)(2,1)S(1)} %get-tuple-element.48.piece_ref.refs_0_, ...), custom_call_target="tpu_custom_call" | custom-call | tf_op jit(solution)/shard_map/document_heads/pallas_call | solution.py:343
  43.8 4.2 %document_heads.3 = (bf16[256,4096]{1,0:T(8,128)(2,1)}, bf16[4096,512]{1,0:T(8,128)(2,1)S(1)}) custom-call(s32[3]{0:T(128)S(1)} %pad_add_fusion.place_ref, bf16[256,4096]{1,0:T(8,128)(2,1)} %query_ref.5, bf16[512,128]{1,0:T(8,128)(2,1)S(1)} %get-tuple-element.36.refs_0_, ...), custom_call_target="tpu_custom_call", output_to_operand_aliasing={{0}: (8, {})} | custom-call | tf_op jit(solution)/shard_map/document_heads/pallas_call | solution.py:343
  48.1 1.3 %project.1 = (f32[64,512]{1,0:T(8,128)S(1)}, bf16[64,512]{1,0:T(8,128)(2,1)S(1)}) custom-call(s32[3]{0:T(128)S(1)} %pad_add_fusion.place_ref, bf16[4096,512]{1,0:T(8,128)(2,1)S(1)} %get-tuple-element.67.weight_ref, bf16[256,128]{1,0:T(8,128)(2,1)S(1)} %merge_parts.1.refs_0_, bf16[256,128]{1,0:T(8,128)(2,1)S(1)} %collective-permute-done.11.refs_1_, ...), custom_call_target="tpu_custom_call" | custom-call | tf_op jit(solution)/shard_map/project/pallas_call | solution.py:238
  49.4 5.3 %collective-permute-start.17 = (bf16[64,512]{1,0:T(8,128)(2,1)S(1)}, bf16[64,512]{1,0:T(8,128)(2,1)S(1)}, u32[]{:S(2)}, u32[]{:S(2)}) collective-permute-start(bf16[64,512]{1,0:T(8,128)(2,1)S(1)} %get-tuple-element.69), channel_id=1, source_target_pairs={{0,1},{1,0},{2,3},{3,2},{4,5},{5,4},{6,7},{7,6},{8,9},{9,8},{10,11... | collective-permute-start | bytes 196616 | tf_op jit(solution)/shard_map/ppermute | solution.py:360
  54.6 0.9 %collective-permute-done.17 = bf16[64,512]{1,0:T(8,128)(2,1)S(1)} collective-permute-done((bf16[64,512]{1,0:T(8,128)(2,1)S(1)}, bf16[64,512]{1,0:T(8,128)(2,1)S(1)}, u32[]{:S(2)}, u32[]{:S(2)}) %collective-permute-start.17) | collective-permute-done | bytes 65568 | tf_op jit(solution)/shard_map/ppermute | solution.py:360
  55.5 0.6 %add_convert_fusion = bf16[64,512]{1,0:T(8,128)(2,1)} fusion(f32[64,512]{1,0:T(8,128)S(1)} %get-tuple-element.68, bf16[64,512]{1,0:T(8,128)(2,1)S(1)} %collective-permute-done.17), kind=kLoop, calls=%fused_computation.1 | loop fusion | flops 98304 | bytes 262144 | tf_op jit(solution)/shard_map/convert_element_type | solution.py:510
  (20 shorter events, 0.2 us)
Async XLA Ops:
  2.4 5.3 %collective-permute-start = (bf16[512,128]{1,0:T(8,128)(2,1)S(1)}, bf16[512,128]{1,0:T(8,128)(2,1)S(1)}, u32[]{:S(2)}, u32[]{:S(2)}) collective-permute-start(bf16[512,128]{1,0:T(8,128)(2,1)S(1)} %get-tuple-element.39.refs_1_), channel_id=1, source_target_pairs={{0,2},{2,0},{4,6},{6,4},{8,10},{10,8},{12,14},{14,12},{16,18},{18,... | collective-permute-start | bytes 393224 | tf_op jit(solution)/shard_map/ppermute | solution.py:360
  4.5 4.1 %collective-permute-start.1 = (bf16[512,128]{1,0:T(8,128)(2,1)S(1)}, bf16[512,128]{1,0:T(8,128)(2,1)S(1)}, u32[]{:S(2)}, u32[]{:S(2)}) collective-permute-start(bf16[512,128]{1,0:T(8,128)(2,1)S(1)} %get-tuple-element.36.refs_0_), channel_id=1, source_target_pairs={{0,4},{2,6},{4,0},{6,2},{8,12},{10,14},{12,8},{14,10},{16,20},{18,... | collective-permute-start | bytes 393224 | tf_op jit(solution)/shard_map/ppermute | solution.py:360
  5.8 5.5 %collective-permute-start.2 = (bf16[512,128]{1,0:T(8,128)(2,1)S(1)}, bf16[512,128]{1,0:T(8,128)(2,1)S(1)}, u32[]{:S(2)}, u32[]{:S(2)}) collective-permute-start(bf16[512,128]{1,0:T(8,128)(2,1)S(1)} %get-tuple-element.37.refs_1_), channel_id=1, source_target_pairs={{0,6},{2,4},{4,2},{6,0},{8,14},{10,12},{12,10},{14,8},{16,22},{18,... | collective-permute-start | bytes 393224 | tf_op jit(solution)/shard_map/ppermute | solution.py:360
  11.3 10.3 %collective-permute-start.6 = (bf16[512,128]{1,0:T(8,128)(2,1)S(1)}, bf16[512,128]{1,0:T(8,128)(2,1)S(1)}, u32[]{:S(2)}, u32[]{:S(2)}) collective-permute-start(bf16[512,128]{1,0:T(8,128)(2,1)S(1)} %select_select_fusion), channel_id=1, source_target_pairs={{0,16},{2,18},{4,20},{6,22},{1,17},{3,19},{5,21},{7,23}} | collective-permute-start | bytes 393224 | tf_op jit(solution)/shard_map/ppermute | solution.py:446
  18.0 3.6 %collective-permute-start.3 = (bf16[272,128]{1,0:T(8,128)(2,1)S(1)}, bf16[272,128]{1,0:T(8,128)(2,1)S(1)}, u32[]{:S(2)}, u32[]{:S(2)}) collective-permute-start(bf16[272,128]{1,0:T(8,128)(2,1)S(1)} %get-tuple-element.53), channel_id=1, source_target_pairs={{0,8},{2,10},{4,12},{6,14},{8,0},{10,2},{12,4},{14,6},{16,24},{18,... | collective-permute-start | bytes 208904 | tf_op jit(solution)/shard_map/ppermute | solution.py:360
  18.1 4.1 %collective-permute-start.4 = (bf16[272,128]{1,0:T(8,128)(2,1)S(1)}, bf16[272,128]{1,0:T(8,128)(2,1)S(1)}, u32[]{:S(2)}, u32[]{:S(2)}) collective-permute-start(bf16[272,128]{1,0:T(8,128)(2,1)S(1)} %get-tuple-element.54), channel_id=1, source_target_pairs={{0,16},{2,18},{4,20},{6,22},{8,24},{10,26},{12,28},{14,30},{16,0},... | collective-permute-start | bytes 208904 | tf_op jit(solution)/shard_map/ppermute | solution.py:360
  18.2 6.2 %collective-permute-start.5 = (bf16[272,128]{1,0:T(8,128)(2,1)S(1)}, bf16[272,128]{1,0:T(8,128)(2,1)S(1)}, u32[]{:S(2)}, u32[]{:S(2)}) collective-permute-start(bf16[272,128]{1,0:T(8,128)(2,1)S(1)} %get-tuple-element.55), channel_id=1, source_target_pairs={{0,24},{2,26},{4,28},{6,30},{8,16},{10,18},{12,20},{14,22},{16,8},... | collective-permute-start | bytes 208904 | tf_op jit(solution)/shard_map/ppermute | solution.py:360
  24.9 6.3 %collective-permute-start.11 = (bf16[256,128]{1,0:T(8,128)(2,1)S(1)}, bf16[256,128]{1,0:T(8,128)(2,1)S(1)}, u32[]{:S(2)}, u32[]{:S(2)}) collective-permute-start(bf16[256,128]{1,0:T(8,128)(2,1)S(1)} %merge_parts.1.refs_0_), channel_id=1, source_target_pairs={{0,8},{2,10},{4,12},{6,14},{8,0},{10,2},{12,4},{14,6},{16,24},{18,... | collective-permute-start | bytes 196616 | tf_op jit(solution)/shard_map/ppermute | solution.py:360
  25.9 5.2 %collective-permute-start.7 = (bf16[512,128]{1,0:T(8,128)(2,1)S(1)}, bf16[512,128]{1,0:T(8,128)(2,1)S(1)}, u32[]{:S(2)}, u32[]{:S(2)}) collective-permute-start(bf16[512,128]{1,0:T(8,128)(2,1)S(1)} %broadcast_select_fusion), channel_id=1, source_target_pairs={{0,8},{2,10},{4,12},{6,14},{16,24},{18,26},{20,28},{22,30},{1,9},{... | collective-permute-start | bytes 393224 | tf_op jit(solution)/shard_map/ppermute | solution.py:446
  28.4 4.4 %collective-permute-start.12 = (bf16[256,128]{1,0:T(8,128)(2,1)S(1)}, bf16[256,128]{1,0:T(8,128)(2,1)S(1)}, u32[]{:S(2)}, u32[]{:S(2)}) collective-permute-start(bf16[256,128]{1,0:T(8,128)(2,1)S(1)} %merge_parts.1.refs_0_), channel_id=1, source_target_pairs={{0,16},{2,18},{4,20},{6,22},{8,24},{10,26},{12,28},{14,30},{16,0},... | collective-permute-start | bytes 196616 | tf_op jit(solution)/shard_map/ppermute | solution.py:360
  31.2 5.3 %collective-permute-start.13 = (bf16[256,128]{1,0:T(8,128)(2,1)S(1)}, bf16[256,128]{1,0:T(8,128)(2,1)S(1)}, u32[]{:S(2)}, u32[]{:S(2)}) collective-permute-start(bf16[256,128]{1,0:T(8,128)(2,1)S(1)} %merge_parts.1.refs_0_), channel_id=1, source_target_pairs={{0,24},{2,26},{4,28},{6,30},{8,16},{10,18},{12,20},{14,22},{16,8},... | collective-permute-start | bytes 196616 | tf_op jit(solution)/shard_map/ppermute | solution.py:360
  31.2 6.8 %collective-permute-start.10 = (bf16[768,128]{1,0:T(8,128)(2,1)S(1)}, bf16[768,128]{1,0:T(8,128)(2,1)S(1)}, u32[]{:S(2)}, u32[]{:S(2)}) collective-permute-start(bf16[768,128]{1,0:T(8,128)(2,1)S(1)} %pad_maximum_fusion), channel_id=1, source_target_pairs={{0,2},{2,0},{4,6},{6,4},{8,10},{10,8},{12,14},{14,12},{16,18},{18,... | collective-permute-start | bytes 589832 | tf_op jit(solution)/shard_map/ppermute | solution.py:360
  32.8 10.9 %collective-permute-start.8 = (bf16[768,128]{1,0:T(8,128)(2,1)S(1)}, bf16[768,128]{1,0:T(8,128)(2,1)S(1)}, u32[]{:S(2)}, u32[]{:S(2)}) collective-permute-start(bf16[768,128]{1,0:T(8,128)(2,1)S(1)} %pad_maximum_fusion), channel_id=1, source_target_pairs={{0,4},{2,6},{4,0},{6,2},{8,12},{10,14},{12,8},{14,10},{16,20},{18,... | collective-permute-start | bytes 589832 | tf_op jit(solution)/shard_map/ppermute | solution.py:360
  33.3 10.5 %collective-permute-start.9 = (bf16[768,128]{1,0:T(8,128)(2,1)S(1)}, bf16[768,128]{1,0:T(8,128)(2,1)S(1)}, u32[]{:S(2)}, u32[]{:S(2)}) collective-permute-start(bf16[768,128]{1,0:T(8,128)(2,1)S(1)} %pad_maximum_fusion), channel_id=1, source_target_pairs={{0,6},{2,4},{4,2},{6,0},{8,14},{10,12},{12,10},{14,8},{16,22},{18,... | collective-permute-start | bytes 589832 | tf_op jit(solution)/shard_map/ppermute | solution.py:360
  36.5 11.6 %collective-permute-start.14 = (bf16[768,128]{1,0:T(8,128)(2,1)S(1)}, bf16[768,128]{1,0:T(8,128)(2,1)S(1)}, u32[]{:S(2)}, u32[]{:S(2)}) collective-permute-start(bf16[768,128]{1,0:T(8,128)(2,1)S(1)} %constant_dynamic-update-slice_fusion), channel_id=1, source_target_pairs={{0,2},{2,0},{4,6},{6,4},{8,10},{10,8},{12,14},{14,12},{16,18},{18,... | collective-permute-start | bytes 589832 | tf_op jit(solution)/shard_map/ppermute | solution.py:360
  37.5 10.6 %collective-permute-start.15 = (bf16[768,128]{1,0:T(8,128)(2,1)S(1)}, bf16[768,128]{1,0:T(8,128)(2,1)S(1)}, u32[]{:S(2)}, u32[]{:S(2)}) collective-permute-start(bf16[768,128]{1,0:T(8,128)(2,1)S(1)} %constant_dynamic-update-slice_fusion), channel_id=1, source_target_pairs={{0,4},{2,6},{4,0},{6,2},{8,12},{10,14},{12,8},{14,10},{16,20},{18,... | collective-permute-start | bytes 589832 | tf_op jit(solution)/shard_map/ppermute | solution.py:360
  38.0 10.1 %collective-permute-start.16 = (bf16[768,128]{1,0:T(8,128)(2,1)S(1)}, bf16[768,128]{1,0:T(8,128)(2,1)S(1)}, u32[]{:S(2)}, u32[]{:S(2)}) collective-permute-start(bf16[768,128]{1,0:T(8,128)(2,1)S(1)} %constant_dynamic-update-slice_fusion), channel_id=1, source_target_pairs={{0,6},{2,4},{4,2},{6,0},{8,14},{10,12},{12,10},{14,8},{16,22},{18,... | collective-permute-start | bytes 589832 | tf_op jit(solution)/shard_map/ppermute | solution.py:360
  49.4 6.2 %collective-permute-start.17 = (bf16[64,512]{1,0:T(8,128)(2,1)S(1)}, bf16[64,512]{1,0:T(8,128)(2,1)S(1)}, u32[]{:S(2)}, u32[]{:S(2)}) collective-permute-start(bf16[64,512]{1,0:T(8,128)(2,1)S(1)} %get-tuple-element.69), channel_id=1, source_target_pairs={{0,1},{1,0},{2,3},{3,2},{4,5},{5,4},{6,7},{7,6},{8,9},{9,8},{10,11... | collective-permute-start | bytes 196616 | tf_op jit(solution)/shard_map/ppermute | solution.py:360

commit v4 on v3

--- a/solution.py
+++ b/solution.py
@@ -44,13 +44,13 @@
     return pltpu.with_memory_space_constraint(values, pltpu.MemorySpace.HBM)
 
 
-def cut_pieces(place, keys, values, group):
+def cut_pieces(place, keys, values, steps):
     token_count = keys.shape[0]
 
     def kernel(place_ref, keys_ref, values_ref, *refs):
         pieces, sems = refs[:-1], refs[-1]
         pairs = []
-        for step, piece in enumerate(pieces):
+        for step, piece in zip(steps, pieces):
             cut = columns(place_ref[0] ^ step, HEAD_SIZE)
             for half, source in enumerate((keys_ref, values_ref)):
                 pairs.append((source.at[:, cut], piece.at[pl.ds(half * token_count, token_count)]))
@@ -66,10 +66,10 @@
     shape = jax.ShapeDtypeStruct((2 * token_count, HEAD_SIZE), keys.dtype)
     return pl.pallas_call(
         kernel,
-        out_shape=[shape] * group,
+        out_shape=[shape] * len(steps),
         in_specs=[SMEM, ANY, ANY],
-        out_specs=[ANY] * group,
-        scratch_shapes=[pltpu.SemaphoreType.DMA((2 * group,))],
+        out_specs=[ANY] * len(steps),
+        scratch_shapes=[pltpu.SemaphoreType.DMA((2 * len(steps),))],
         compiler_params=PARAMS,
         name="cut_pieces",
     )(place, in_hbm(keys), in_hbm(values))
@@ -89,16 +89,25 @@
     return [jax.ShapeDtypeStruct(shape, query.dtype)] * len(steps)
 
 
-def bring_queries(place, query, group, steps, question, piece):
+def bring_queries(place, query, group, steps, question, piece, keys, values):
     count = len(steps)
 
-    def kernel(place_ref, query_ref, piece_ref, *refs):
+    def kernel(place_ref, query_ref, piece_ref, keys_ref, values_ref, *refs):
         question_refs, refs = refs[: len(question)], refs[len(question) :]
-        targets, sems = refs[:-1], refs[-1]
+        targets, own, sems = refs[:-2], refs[-2], refs[-1]
         copies = query_copies(place_ref[0], query_ref, steps, targets[:count], sems)
         for at, (source, target) in enumerate(zip(question_refs, targets[count:])):
             cut = columns(place_ref[0], target.shape[1])
             copies.append(pltpu.make_async_copy(source.at[:, cut], target, sems.at[count + at]))
+        rows = keys.shape[0]
+        for half, source in enumerate((keys_ref, values_ref)):
+            copies.append(
+                pltpu.make_async_copy(
+                    source.at[:, columns(place_ref[0], HEAD_SIZE)],
+                    own.at[pl.ds(half * rows, rows)],
+                    sems.at[count + len(question) + half],
+                )
+            )
         for copy in copies:
             copy.start()
         for copy in copies:
@@ -109,15 +118,16 @@
         shapes.append(
             jax.ShapeDtypeStruct((array.shape[0], array.shape[1] // group), array.dtype)
         )
+    shapes.append(jax.ShapeDtypeStruct(piece.shape, piece.dtype))
     return pl.pallas_call(
         kernel,
         out_shape=shapes,
-        in_specs=[SMEM, ANY, ANY] + [ANY] * len(question),
+        in_specs=[SMEM, ANY, ANY, ANY, ANY] + [ANY] * len(question),
         out_specs=[ANY] * len(shapes),
-        scratch_shapes=[pltpu.SemaphoreType.DMA((len(shapes),))],
+        scratch_shapes=[pltpu.SemaphoreType.DMA((len(shapes) + 1,))],
         compiler_params=PARAMS,
         name="bring_queries",
-    )(place, in_hbm(query), piece, *map(in_hbm, question))
+    )(place, in_hbm(query), piece, in_hbm(keys), in_hbm(values), *map(in_hbm, question))
 
 
 def question_parts(place, query, own_keys, own_values, pieces, ring):
@@ -422,18 +432,30 @@
     def in_ring(values, step):
         return swapped(values, "ctx", ctx_size, step * group)
 
-    whole_units = head_total % ctx_size == 0
+    whole_units = head_total % ctx_size == 0 and group > 1
     question = (question_query, prompt_keys, prompt_values) if whole_units else ()
-    own_pieces = cut_pieces(place, document_keys, document_values, group)
-    pieces = own_pieces
-    pieces = [pieces[0]] + [in_group(pieces[step], step) for step in range(1, group)]
+    sent = range(1, group) if whole_units else range(group)
+    own_pieces = list(cut_pieces(place, document_keys, document_values, sent))
+    if whole_units:
+        own_pieces.insert(0, None)
+    pieces = [own_pieces[0]] + [in_group(own_pieces[step], step) for step in range(1, group)]
 
     half = max(1, group // 2)
     near = ()
     if whole_units:
-        near = bring_queries(place, document_query, group, range(half), question, own_pieces[0])
-        pieces, near = lax.optimization_barrier((pieces, near))
-        near, question = near[:half], near[half:]
+        near = bring_queries(
+            place,
+            document_query,
+            group,
+            range(half),
+            question,
+            own_pieces[1],
+            document_keys,
+            document_values,
+        )
+        arrived, near = lax.optimization_barrier((pieces[1:], near))
+        near, question, own_pieces[0] = near[:half], near[half:-1], near[-1]
+        pieces = [own_pieces[0], *arrived]
 
     anchor = lax.select_n(member, *pieces) if group > 1 else pieces[0]
 

time: 56.8 us -> 56.7 us (level)
  no operation moved by 1% of the time
where the time goes in v4:
time: 56.7 us; the launch traced here: 56.1 us
  starting transfers between devices  28.7 us (51%)
  Pallas kernels  16.5 us (29%)
  waiting for transfers between devices  9.21 us (16%)
  between operations  0.87 us (2%)
  other arithmetic  0.8 us (1%)
    ppermute x16, starting transfers between devices, swapped(): lax.ppermute(values, axis, [(place, place ^ step) for place in range(size)])  22 us
    ppermute x16, waiting for transfers between devices, swapped(): lax.ppermute(values, axis, [(place, place ^ step) for place in range(size)])  9.2 us
    pallas_call x2, Pallas kernels, document_heads(): pl.pallas_call(kernel, out_shape=out_shape, in_specs=[SMEM, ANY] + [VMEM]...  8.83 us
    ppermute x2, starting transfers between devices, sent_on(): arrived = lax.ppermute(anchor, 'ctx', pairs)  6.62 us
    pallas_call x1, Pallas kernels, question_parts(): pl.pallas_call(kernel, out_shape=[jax.ShapeDtypeStruct(out_shape, jnp.bfl...  2.42 us
    pallas_call x1, Pallas kernels, bring_queries(): pl.pallas_call(kernel, out_shape=shapes, in_specs=[SMEM, ANY, ANY, ANY, A...  1.9 us
    pallas_call x1, Pallas kernels, cut_pieces(): pl.pallas_call(kernel, out_shape=[shape] * len(steps), in_specs=[SMEM, AN...  1.61 us
    pallas_call x1, Pallas kernels, project(): pl.pallas_call(kernel, out_shape=[jax.ShapeDtypeStruct((row_count // spli...  1.28 us
  transfers between devices with their start and end apart: 18, of which 8 were waited for; matrix products, arithmetic and copies ran while one was open for 0% of the time, Pallas kernels for 23%

profile of v4, /device:TPU:1, one launch (start us, length us, event | category | flops | bytes accessed | tf_op | source)
XLA Modules:
  0.0 56.1 jit_solution(16308380463029530248)
XLA Ops:
  0.7 0.1 pad_add_fusion.place_ref
  0.7 1.6 %cut_pieces.1 = (bf16[512,128]{1,0:T(8,128)(2,1)S(1)}, bf16[512,128]{1,0:T(8,128)(2,1)S(1)}, bf16[512,128]{1,0:T(8,128)(2,1)S(1)}) custom-call(s32[3]{0:T(128)S(1)} %pad_add_fusion.place_ref, bf16[256,512]{1,0:T(8,128)(2,1)} %keys_ref.3, bf16[256,512]{1,0:T(8,128)(2,1)} %values_ref.3), custom_call_target="tpu_custom_call" | custom-call | tf_op jit(solution)/shard_map/cut_pieces/pallas_call | solution.py:67
  2.3 2.1 %collective-permute-start = (bf16[512,128]{1,0:T(8,128)(2,1)S(1)}, bf16[512,128]{1,0:T(8,128)(2,1)S(1)}, u32[]{:S(2)}, u32[]{:S(2)}) collective-permute-start(bf16[512,128]{1,0:T(8,128)(2,1)S(1)} %get-tuple-element.38.piece_ref.refs_1_), channel_id=1, source_target_pairs={{0,2},{2,0},{4,6},{6,4},{8,10},{10,8},{12,14},{14,12},{16,18},{18,... | collective-permute-start | bytes 393224 | tf_op jit(solution)/shard_map/ppermute | solution.py:370
  4.4 1.2 %collective-permute-start.1 = (bf16[512,128]{1,0:T(8,128)(2,1)S(1)}, bf16[512,128]{1,0:T(8,128)(2,1)S(1)}, u32[]{:S(2)}, u32[]{:S(2)}) collective-permute-start(bf16[512,128]{1,0:T(8,128)(2,1)S(1)} %get-tuple-element.36.refs_0_), channel_id=1, source_target_pairs={{0,4},{2,6},{4,0},{6,2},{8,12},{10,14},{12,8},{14,10},{16,20},{18,... | collective-permute-start | bytes 393224 | tf_op jit(solution)/shard_map/ppermute | solution.py:370
  5.7 1.9 %bring_queries.1 = (bf16[256,1024]{1,0:T(8,128)(2,1)S(1)}, bf16[256,1024]{1,0:T(8,128)(2,1)S(1)}, bf16[128,1024]{1,0:T(8,128)(2,1)S(1)}, bf16[128,128]{1,0:T(8,1...) custom-call(s32[3]{0:T(128)S(1)} %pad_add_fusion.place_ref, bf16[256,4096]{1,0:T(8,128)(2,1)} %query_ref.5, ...), custom_call_target="tpu_custom_call" | custom-call | tf_op jit(solution)/shard_map/bring_queries/pallas_call | solution.py:122
  7.7 0.9 %collective-permute-done.1.refs_2_ = bf16[512,128]{1,0:T(8,128)(2,1)S(1)} collective-permute-done((bf16[512,128]{1,0:T(8,128)(2,1)S(1)}, bf16[512,128]{1,0:T(8,128)(2,1)S(1)}, u32[]{:S(2)}, u32[]{:S(2)}) %collective-permute-start.1) | collective-permute-done | bytes 131104 | tf_op jit(solution)/shard_map/ppermute | solution.py:370
  8.6 2.7 %collective-permute-done.2.refs_3_ = bf16[512,128]{1,0:T(8,128)(2,1)S(1)} collective-permute-done((bf16[512,128]{1,0:T(8,128)(2,1)S(1)}, bf16[512,128]{1,0:T(8,128)(2,1)S(1)}, u32[]{:S(2)}, u32[]{:S(2)}) %collective-permute-start.2) | collective-permute-done | bytes 131104 | tf_op jit(solution)/shard_map/ppermute | solution.py:370
  11.2 4.2 %collective-permute-start.6 = (bf16[512,128]{1,0:T(8,128)(2,1)S(1)}, bf16[512,128]{1,0:T(8,128)(2,1)S(1)}, u32[]{:S(2)}, u32[]{:S(2)}) collective-permute-start(bf16[512,128]{1,0:T(8,128)(2,1)S(1)} %select_select_fusion), channel_id=1, source_target_pairs={{0,16},{2,18},{4,20},{6,22},{1,17},{3,19},{5,21},{7,23}} | collective-permute-start | bytes 393224 | tf_op jit(solution)/shard_map/ppermute | solution.py:468
  15.5 2.4 %question_parts.1 = (bf16[272,128]{1,0:T(8,128)(2,1)S(1)}, bf16[272,128]{1,0:T(8,128)(2,1)S(1)}, bf16[272,128]{1,0:T(8,128)(2,1)S(1)}, bf16[272,128]{1,0:T(8,128)(2,1)S(1)}) custom-call(s32[3]{0:T(128)S(1)} %pad_add_fusion.place_ref, bf16[128,1024]{1,0:T(8,128)(2,1)S(1)} %get-tuple-element.45.query_ref, bf16[128,128]{1,0:T(8,128)(2,1)S(1)} %get-tuple-element.46.own_keys_ref, ...), custom_call_target="tpu_custom_call" | custom-call | tf_op jit(solution)/shard_map/question_parts/pallas_call | solution.py:179
  17.9 0.1 collective-permute-start.3
  18.0 0.1 collective-permute-start.4
  18.1 3.5 %collective-permute-start.5 = (bf16[272,128]{1,0:T(8,128)(2,1)S(1)}, bf16[272,128]{1,0:T(8,128)(2,1)S(1)}, u32[]{:S(2)}, u32[]{:S(2)}) collective-permute-start(bf16[272,128]{1,0:T(8,128)(2,1)S(1)} %get-tuple-element.55), channel_id=1, source_target_pairs={{0,24},{2,26},{4,28},{6,30},{8,16},{10,18},{12,20},{14,22},{16,8},... | collective-permute-start | bytes 208904 | tf_op jit(solution)/shard_map/ppermute | solution.py:370
  21.6 0.6 collective-permute-done.4.refs_2_
  22.1 2.2 %collective-permute-done.5.refs_3_ = bf16[272,128]{1,0:T(8,128)(2,1)S(1)} collective-permute-done((bf16[272,128]{1,0:T(8,128)(2,1)S(1)}, bf16[272,128]{1,0:T(8,128)(2,1)S(1)}, u32[]{:S(2)}, u32[]{:S(2)}) %collective-permute-start.5) | collective-permute-done | bytes 69664 | tf_op jit(solution)/shard_map/ppermute | solution.py:370
  24.3 0.5 merge_parts.1.refs_0_
  24.8 1.0 %collective-permute-start.11 = (bf16[256,128]{1,0:T(8,128)(2,1)S(1)}, bf16[256,128]{1,0:T(8,128)(2,1)S(1)}, u32[]{:S(2)}, u32[]{:S(2)}) collective-permute-start(bf16[256,128]{1,0:T(8,128)(2,1)S(1)} %merge_parts.1.refs_0_), channel_id=1, source_target_pairs={{0,8},{2,10},{4,12},{6,14},{8,0},{10,2},{12,4},{14,6},{16,24},{18,... | collective-permute-start | bytes 196616 | tf_op jit(solution)/shard_map/ppermute | solution.py:370
  25.9 2.4 %collective-permute-start.7 = (bf16[512,128]{1,0:T(8,128)(2,1)S(1)}, bf16[512,128]{1,0:T(8,128)(2,1)S(1)}, u32[]{:S(2)}, u32[]{:S(2)}) collective-permute-start(bf16[512,128]{1,0:T(8,128)(2,1)S(1)} %broadcast_select_fusion), channel_id=1, source_target_pairs={{0,8},{2,10},{4,12},{6,14},{16,24},{18,26},{20,28},{22,30},{1,9},{... | collective-permute-start | bytes 393224 | tf_op jit(solution)/shard_map/ppermute | solution.py:468
  28.3 2.8 %collective-permute-start.12 = (bf16[256,128]{1,0:T(8,128)(2,1)S(1)}, bf16[256,128]{1,0:T(8,128)(2,1)S(1)}, u32[]{:S(2)}, u32[]{:S(2)}) collective-permute-start(bf16[256,128]{1,0:T(8,128)(2,1)S(1)} %merge_parts.1.refs_0_), channel_id=1, source_target_pairs={{0,16},{2,18},{4,20},{6,22},{8,24},{10,26},{12,28},{14,30},{16,0},... | collective-permute-start | bytes 196616 | tf_op jit(solution)/shard_map/ppermute | solution.py:370
  31.1 1.0 %collective-permute-start.10 = (bf16[768,128]{1,0:T(8,128)(2,1)S(1)}, bf16[768,128]{1,0:T(8,128)(2,1)S(1)}, u32[]{:S(2)}, u32[]{:S(2)}) collective-permute-start(bf16[768,128]{1,0:T(8,128)(2,1)S(1)} %pad_maximum_fusion), channel_id=1, source_target_pairs={{0,2},{2,0},{4,6},{6,4},{8,10},{10,8},{12,14},{14,12},{16,18},{18,... | collective-permute-start | bytes 589832 | tf_op jit(solution)/shard_map/ppermute | solution.py:370
  32.2 0.5 collective-permute-done.12.refs_2_
  32.7 0.5 collective-permute-start.8
  33.2 1.7 %collective-permute-start.9 = (bf16[768,128]{1,0:T(8,128)(2,1)S(1)}, bf16[768,128]{1,0:T(8,128)(2,1)S(1)}, u32[]{:S(2)}, u32[]{:S(2)}) collective-permute-start(bf16[768,128]{1,0:T(8,128)(2,1)S(1)} %pad_maximum_fusion), channel_id=1, source_target_pairs={{0,6},{2,4},{4,2},{6,0},{8,14},{10,12},{12,10},{14,8},{16,22},{18,... | collective-permute-start | bytes 589832 | tf_op jit(solution)/shard_map/ppermute | solution.py:370
  35.0 1.4 %collective-permute-done.13.refs_3_ = bf16[256,128]{1,0:T(8,128)(2,1)S(1)} collective-permute-done((bf16[256,128]{1,0:T(8,128)(2,1)S(1)}, bf16[256,128]{1,0:T(8,128)(2,1)S(1)}, u32[]{:S(2)}, u32[]{:S(2)}) %collective-permute-start.13) | collective-permute-done | bytes 65568 | tf_op jit(solution)/shard_map/ppermute | solution.py:370
  36.4 1.0 %collective-permute-start.14 = (bf16[768,128]{1,0:T(8,128)(2,1)S(1)}, bf16[768,128]{1,0:T(8,128)(2,1)S(1)}, u32[]{:S(2)}, u32[]{:S(2)}) collective-permute-start(bf16[768,128]{1,0:T(8,128)(2,1)S(1)} %constant_dynamic-update-slice_fusion), channel_id=1, source_target_pairs={{0,2},{2,0},{4,6},{6,4},{8,10},{10,8},{12,14},{14,12},{16,18},{18,... | collective-permute-start | bytes 589832 | tf_op jit(solution)/shard_map/ppermute | solution.py:370
  37.4 0.5 collective-permute-start.15
  37.9 1.2 %collective-permute-start.16 = (bf16[768,128]{1,0:T(8,128)(2,1)S(1)}, bf16[768,128]{1,0:T(8,128)(2,1)S(1)}, u32[]{:S(2)}, u32[]{:S(2)}) collective-permute-start(bf16[768,128]{1,0:T(8,128)(2,1)S(1)} %constant_dynamic-update-slice_fusion), channel_id=1, source_target_pairs={{0,6},{2,4},{4,2},{6,0},{8,14},{10,12},{12,10},{14,8},{16,22},{18,... | collective-permute-start | bytes 589832 | tf_op jit(solution)/shard_map/ppermute | solution.py:370
  39.1 4.6 %document_heads.2 = (bf16[256,4096]{1,0:T(8,128)(2,1)}, bf16[256,1024]{1,0:T(8,128)(2,1)S(1)}, bf16[256,1024]{1,0:T(8,128)(2,1)S(1)}) custom-call(s32[3]{0:T(128)S(1)} %pad_add_fusion.place_ref, bf16[256,4096]{1,0:T(8,128)(2,1)} %query_ref.5, bf16[512,128]{1,0:T(8,128)(2,1)S(1)} %get-tuple-element.48.refs_0_, ...), custom_call_target="tpu_custom_call" | custom-call | tf_op jit(solution)/shard_map/document_heads/pallas_call | solution.py:353
  43.7 4.2 %document_heads.3 = (bf16[256,4096]{1,0:T(8,128)(2,1)}, bf16[4096,512]{1,0:T(8,128)(2,1)S(1)}) custom-call(s32[3]{0:T(128)S(1)} %pad_add_fusion.place_ref, bf16[256,4096]{1,0:T(8,128)(2,1)} %query_ref.5, bf16[512,128]{1,0:T(8,128)(2,1)S(1)} %get-tuple-element.36.refs_0_, ...), custom_call_target="tpu_custom_call", output_to_operand_aliasing={{0}: (8, {})} | custom-call | tf_op jit(solution)/shard_map/document_heads/pallas_call | solution.py:353
  48.0 1.3 %project.1 = (f32[64,512]{1,0:T(8,128)S(1)}, bf16[64,512]{1,0:T(8,128)(2,1)S(1)}) custom-call(s32[3]{0:T(128)S(1)} %pad_add_fusion.place_ref, bf16[4096,512]{1,0:T(8,128)(2,1)S(1)} %get-tuple-element.67.weight_ref, bf16[256,128]{1,0:T(8,128)(2,1)S(1)} %merge_parts.1.refs_0_, bf16[256,128]{1,0:T(8,128)(2,1)S(1)} %collective-permute-done.11.refs_1_, ...), custom_call_target="tpu_custom_call" | custom-call | tf_op jit(solution)/shard_map/project/pallas_call | solution.py:248
  49.3 5.3 %collective-permute-start.17 = (bf16[64,512]{1,0:T(8,128)(2,1)S(1)}, bf16[64,512]{1,0:T(8,128)(2,1)S(1)}, u32[]{:S(2)}, u32[]{:S(2)}) collective-permute-start(bf16[64,512]{1,0:T(8,128)(2,1)S(1)} %get-tuple-element.69), channel_id=1, source_target_pairs={{0,1},{1,0},{2,3},{3,2},{4,5},{5,4},{6,7},{7,6},{8,9},{9,8},{10,11... | collective-permute-start | bytes 196616 | tf_op jit(solution)/shard_map/ppermute | solution.py:370
  54.5 0.9 %collective-permute-done.17 = bf16[64,512]{1,0:T(8,128)(2,1)S(1)} collective-permute-done((bf16[64,512]{1,0:T(8,128)(2,1)S(1)}, bf16[64,512]{1,0:T(8,128)(2,1)S(1)}, u32[]{:S(2)}, u32[]{:S(2)}) %collective-permute-start.17) | collective-permute-done | bytes 65568 | tf_op jit(solution)/shard_map/ppermute | solution.py:370
  55.4 0.6 %add_convert_fusion = bf16[64,512]{1,0:T(8,128)(2,1)} fusion(f32[64,512]{1,0:T(8,128)S(1)} %get-tuple-element.68, bf16[64,512]{1,0:T(8,128)(2,1)S(1)} %collective-permute-done.17), kind=kLoop, calls=%fused_computation.1 | loop fusion | flops 98304 | bytes 262144 | tf_op jit(solution)/shard_map/convert_element_type | solution.py:532
  (20 shorter events, 0.2 us)
Async XLA Ops:
  2.3 5.3 %collective-permute-start = (bf16[512,128]{1,0:T(8,128)(2,1)S(1)}, bf16[512,128]{1,0:T(8,128)(2,1)S(1)}, u32[]{:S(2)}, u32[]{:S(2)}) collective-permute-start(bf16[512,128]{1,0:T(8,128)(2,1)S(1)} %get-tuple-element.38.piece_ref.refs_1_), channel_id=1, source_target_pairs={{0,2},{2,0},{4,6},{6,4},{8,10},{10,8},{12,14},{14,12},{16,18},{18,... | collective-permute-start | bytes 393224 | tf_op jit(solution)/shard_map/ppermute | solution.py:370
  4.4 4.1 %collective-permute-start.1 = (bf16[512,128]{1,0:T(8,128)(2,1)S(1)}, bf16[512,128]{1,0:T(8,128)(2,1)S(1)}, u32[]{:S(2)}, u32[]{:S(2)}) collective-permute-start(bf16[512,128]{1,0:T(8,128)(2,1)S(1)} %get-tuple-element.36.refs_0_), channel_id=1, source_target_pairs={{0,4},{2,6},{4,0},{6,2},{8,12},{10,14},{12,8},{14,10},{16,20},{18,... | collective-permute-start | bytes 393224 | tf_op jit(solution)/shard_map/ppermute | solution.py:370
  5.7 5.5 %collective-permute-start.2 = (bf16[512,128]{1,0:T(8,128)(2,1)S(1)}, bf16[512,128]{1,0:T(8,128)(2,1)S(1)}, u32[]{:S(2)}, u32[]{:S(2)}) collective-permute-start(bf16[512,128]{1,0:T(8,128)(2,1)S(1)} %get-tuple-element.37.refs_1_), channel_id=1, source_target_pairs={{0,6},{2,4},{4,2},{6,0},{8,14},{10,12},{12,10},{14,8},{16,22},{18,... | collective-permute-start | bytes 393224 | tf_op jit(solution)/shard_map/ppermute | solution.py:370
  11.2 10.3 %collective-permute-start.6 = (bf16[512,128]{1,0:T(8,128)(2,1)S(1)}, bf16[512,128]{1,0:T(8,128)(2,1)S(1)}, u32[]{:S(2)}, u32[]{:S(2)}) collective-permute-start(bf16[512,128]{1,0:T(8,128)(2,1)S(1)} %select_select_fusion), channel_id=1, source_target_pairs={{0,16},{2,18},{4,20},{6,22},{1,17},{3,19},{5,21},{7,23}} | collective-permute-start | bytes 393224 | tf_op jit(solution)/shard_map/ppermute | solution.py:468
  17.9 3.6 %collective-permute-start.3 = (bf16[272,128]{1,0:T(8,128)(2,1)S(1)}, bf16[272,128]{1,0:T(8,128)(2,1)S(1)}, u32[]{:S(2)}, u32[]{:S(2)}) collective-permute-start(bf16[272,128]{1,0:T(8,128)(2,1)S(1)} %get-tuple-element.53), channel_id=1, source_target_pairs={{0,8},{2,10},{4,12},{6,14},{8,0},{10,2},{12,4},{14,6},{16,24},{18,... | collective-permute-start | bytes 208904 | tf_op jit(solution)/shard_map/ppermute | solution.py:370
  18.0 4.1 %collective-permute-start.4 = (bf16[272,128]{1,0:T(8,128)(2,1)S(1)}, bf16[272,128]{1,0:T(8,128)(2,1)S(1)}, u32[]{:S(2)}, u32[]{:S(2)}) collective-permute-start(bf16[272,128]{1,0:T(8,128)(2,1)S(1)} %get-tuple-element.54), channel_id=1, source_target_pairs={{0,16},{2,18},{4,20},{6,22},{8,24},{10,26},{12,28},{14,30},{16,0},... | collective-permute-start | bytes 208904 | tf_op jit(solution)/shard_map/ppermute | solution.py:370
  18.1 6.2 %collective-permute-start.5 = (bf16[272,128]{1,0:T(8,128)(2,1)S(1)}, bf16[272,128]{1,0:T(8,128)(2,1)S(1)}, u32[]{:S(2)}, u32[]{:S(2)}) collective-permute-start(bf16[272,128]{1,0:T(8,128)(2,1)S(1)} %get-tuple-element.55), channel_id=1, source_target_pairs={{0,24},{2,26},{4,28},{6,30},{8,16},{10,18},{12,20},{14,22},{16,8},... | collective-permute-start | bytes 208904 | tf_op jit(solution)/shard_map/ppermute | solution.py:370
  24.8 6.3 %collective-permute-start.11 = (bf16[256,128]{1,0:T(8,128)(2,1)S(1)}, bf16[256,128]{1,0:T(8,128)(2,1)S(1)}, u32[]{:S(2)}, u32[]{:S(2)}) collective-permute-start(bf16[256,128]{1,0:T(8,128)(2,1)S(1)} %merge_parts.1.refs_0_), channel_id=1, source_target_pairs={{0,8},{2,10},{4,12},{6,14},{8,0},{10,2},{12,4},{14,6},{16,24},{18,... | collective-permute-start | bytes 196616 | tf_op jit(solution)/shard_map/ppermute | solution.py:370
  25.9 5.2 %collective-permute-start.7 = (bf16[512,128]{1,0:T(8,128)(2,1)S(1)}, bf16[512,128]{1,0:T(8,128)(2,1)S(1)}, u32[]{:S(2)}, u32[]{:S(2)}) collective-permute-start(bf16[512,128]{1,0:T(8,128)(2,1)S(1)} %broadcast_select_fusion), channel_id=1, source_target_pairs={{0,8},{2,10},{4,12},{6,14},{16,24},{18,26},{20,28},{22,30},{1,9},{... | collective-permute-start | bytes 393224 | tf_op jit(solution)/shard_map/ppermute | solution.py:468
  28.3 4.4 %collective-permute-start.12 = (bf16[256,128]{1,0:T(8,128)(2,1)S(1)}, bf16[256,128]{1,0:T(8,128)(2,1)S(1)}, u32[]{:S(2)}, u32[]{:S(2)}) collective-permute-start(bf16[256,128]{1,0:T(8,128)(2,1)S(1)} %merge_parts.1.refs_0_), channel_id=1, source_target_pairs={{0,16},{2,18},{4,20},{6,22},{8,24},{10,26},{12,28},{14,30},{16,0},... | collective-permute-start | bytes 196616 | tf_op jit(solution)/shard_map/ppermute | solution.py:370
  31.1 5.3 %collective-permute-start.13 = (bf16[256,128]{1,0:T(8,128)(2,1)S(1)}, bf16[256,128]{1,0:T(8,128)(2,1)S(1)}, u32[]{:S(2)}, u32[]{:S(2)}) collective-permute-start(bf16[256,128]{1,0:T(8,128)(2,1)S(1)} %merge_parts.1.refs_0_), channel_id=1, source_target_pairs={{0,24},{2,26},{4,28},{6,30},{8,16},{10,18},{12,20},{14,22},{16,8},... | collective-permute-start | bytes 196616 | tf_op jit(solution)/shard_map/ppermute | solution.py:370
  31.1 6.8 %collective-permute-start.10 = (bf16[768,128]{1,0:T(8,128)(2,1)S(1)}, bf16[768,128]{1,0:T(8,128)(2,1)S(1)}, u32[]{:S(2)}, u32[]{:S(2)}) collective-permute-start(bf16[768,128]{1,0:T(8,128)(2,1)S(1)} %pad_maximum_fusion), channel_id=1, source_target_pairs={{0,2},{2,0},{4,6},{6,4},{8,10},{10,8},{12,14},{14,12},{16,18},{18,... | collective-permute-start | bytes 589832 | tf_op jit(solution)/shard_map/ppermute | solution.py:370
  32.7 10.9 %collective-permute-start.8 = (bf16[768,128]{1,0:T(8,128)(2,1)S(1)}, bf16[768,128]{1,0:T(8,128)(2,1)S(1)}, u32[]{:S(2)}, u32[]{:S(2)}) collective-permute-start(bf16[768,128]{1,0:T(8,128)(2,1)S(1)} %pad_maximum_fusion), channel_id=1, source_target_pairs={{0,4},{2,6},{4,0},{6,2},{8,12},{10,14},{12,8},{14,10},{16,20},{18,... | collective-permute-start | bytes 589832 | tf_op jit(solution)/shard_map/ppermute | solution.py:370
  33.2 10.5 %collective-permute-start.9 = (bf16[768,128]{1,0:T(8,128)(2,1)S(1)}, bf16[768,128]{1,0:T(8,128)(2,1)S(1)}, u32[]{:S(2)}, u32[]{:S(2)}) collective-permute-start(bf16[768,128]{1,0:T(8,128)(2,1)S(1)} %pad_maximum_fusion), channel_id=1, source_target_pairs={{0,6},{2,4},{4,2},{6,0},{8,14},{10,12},{12,10},{14,8},{16,22},{18,... | collective-permute-start | bytes 589832 | tf_op jit(solution)/shard_map/ppermute | solution.py:370
  36.4 11.6 %collective-permute-start.14 = (bf16[768,128]{1,0:T(8,128)(2,1)S(1)}, bf16[768,128]{1,0:T(8,128)(2,1)S(1)}, u32[]{:S(2)}, u32[]{:S(2)}) collective-permute-start(bf16[768,128]{1,0:T(8,128)(2,1)S(1)} %constant_dynamic-update-slice_fusion), channel_id=1, source_target_pairs={{0,2},{2,0},{4,6},{6,4},{8,10},{10,8},{12,14},{14,12},{16,18},{18,... | collective-permute-start | bytes 589832 | tf_op jit(solution)/shard_map/ppermute | solution.py:370
  37.4 10.6 %collective-permute-start.15 = (bf16[768,128]{1,0:T(8,128)(2,1)S(1)}, bf16[768,128]{1,0:T(8,128)(2,1)S(1)}, u32[]{:S(2)}, u32[]{:S(2)}) collective-permute-start(bf16[768,128]{1,0:T(8,128)(2,1)S(1)} %constant_dynamic-update-slice_fusion), channel_id=1, source_target_pairs={{0,4},{2,6},{4,0},{6,2},{8,12},{10,14},{12,8},{14,10},{16,20},{18,... | collective-permute-start | bytes 589832 | tf_op jit(solution)/shard_map/ppermute | solution.py:370
  37.9 10.1 %collective-permute-start.16 = (bf16[768,128]{1,0:T(8,128)(2,1)S(1)}, bf16[768,128]{1,0:T(8,128)(2,1)S(1)}, u32[]{:S(2)}, u32[]{:S(2)}) collective-permute-start(bf16[768,128]{1,0:T(8,128)(2,1)S(1)} %constant_dynamic-update-slice_fusion), channel_id=1, source_target_pairs={{0,6},{2,4},{4,2},{6,0},{8,14},{10,12},{12,10},{14,8},{16,22},{18,... | collective-permute-start | bytes 589832 | tf_op jit(solution)/shard_map/ppermute | solution.py:370
  49.3 6.2 %collective-permute-start.17 = (bf16[64,512]{1,0:T(8,128)(2,1)S(1)}, bf16[64,512]{1,0:T(8,128)(2,1)S(1)}, u32[]{:S(2)}, u32[]{:S(2)}) collective-permute-start(bf16[64,512]{1,0:T(8,128)(2,1)S(1)} %get-tuple-element.69), channel_id=1, source_target_pairs={{0,1},{1,0},{2,3},{3,2},{4,5},{5,4},{6,7},{7,6},{8,9},{9,8},{10,11... | collective-permute-start | bytes 196616 | tf_op jit(solution)/shard_map/ppermute | solution.py:370
